TPU v7x, 128 devices: a whole 4x4x4 slice. The times are simulated.
128 devices in a mesh: clu: 128 (over y, x, z, core).
Axes of the slice: x: 4, y: 4, z: 4, core: 2. Of those that a mesh axis runs over, the one named last changes fastest.
Arguments:
- start_vector: float32 [512, 8, 256], P('clu'), may hold values from -6 to 6
- leaf_size: int32 [512], P('clu'), may hold values from 64 to 256, as said below
- diag_blocks: bfloat16 [512, 256, 256], P('clu'), as said below
- near_blocks: bfloat16 [2048, 256, 256], P('clu'), may hold values from -0.09375 to 0.09375
- near_count: int32 [128], P('clu'), may hold values from 12 to 16, as said below
- near_first: int32 [2048], P('clu'), may hold values from 0 to 3
- near_second: int32 [2048], P('clu'), may hold values from 1 to 7, as said below
- leaf_basis: bfloat16 [512, 64, 256], P('clu'), may hold values from -0.375 to 0.375
- transfer: float32 [512, 64, 64], P('clu'), may hold values from -0.5 to 0.5
- coupling: float32 [32768, 64, 64], P('clu'), may hold values from -0.1875 to 0.1875
- send_slot: int32 [128, 256], P('clu'), may hold values from -1 to 5, as said below
- far_target: int32 [128, 256], P('clu'), may hold values from -1 to 5, as said below
Outputs:
- products: float32 [4, 512, 8, 256], P(None, 'clu')
Inputs may be any that keep to these rules, and one draw needn't show every extreme that they name: Positions from leaf_size[l] to 255 of leaf l are padding. Device d uses its first near_count[d] near-field slots, and some device uses all 16. near_second exceeds near_first of the same entry by 1 to 4; values from 4 on name leaves of the next device, and the last device continues at device 0. `send_slot`: for c < 1: a leaf slot (below 4) if devices d and p are at most 8 apart around the axis, else -1. For other c: a parent slot. `far_target`: for c < 1: a leaf slot (below 4) if devices d and p are at most 8 apart around the axis, else -1. For other c: a parent slot. `diag_blocks`: each block is symmetric.
All inputs are finite; a program needn't handle non-finite values.
Results may differ from a plain program's by a relative error of at most 0.01.
Values may be sent and summed in bfloat16 or wider, within the bound.
A program may use at most 128 MiB of HBM per device.

v0:
```python
import jax
import jax.numpy as jnp
from jax import lax
from jax.sharding import PartitionSpec as P

PRODUCTS = 4


def passed_along(value, axis, steps):
    count = lax.axis_size(axis)
    pairs = [(source, (source + steps) % count) for source in range(count)]
    return lax.ppermute(value, axis, pairs)


def on_device(
    start_vector,
    leaf_size,
    diag_blocks,
    near_blocks,
    near_count,
    near_first,
    near_second,
    leaf_basis,
    transfer,
    coupling,
    send_slot,
    far_target,
):
    highest = lax.Precision.HIGHEST
    leaves, rhs_count, points = start_vector.shape
    rank = leaf_basis.shape[1]
    coef_width = rhs_count * rank
    devices = lax.axis_size("clu")
    cluster_slots = leaves + leaves // 2
    per_peer = send_slot.shape[1] // devices
    pair_rows = devices * per_peer
    capacity = near_blocks.shape[0]
    point_ids = jnp.arange(points, dtype=jnp.int32)
    point_mask = (point_ids[None, :] < leaf_size[:, None]).astype(jnp.float32)[:, None, :]
    live_slots = (jnp.arange(capacity, dtype=jnp.int32) < near_count[0]).astype(jnp.float32)
    window = jnp.arange(2 * leaves, dtype=jnp.int32)
    pick_first = (near_first[:, None] == window[None, :]).astype(jnp.float32) * live_slots[:, None]
    pick_second = (near_second[:, None] == window[None, :]).astype(jnp.float32) * live_slots[
        :, None
    ]
    first_bf = pick_first.astype(jnp.bfloat16)
    second_bf = pick_second.astype(jnp.bfloat16)
    slot_ids = jnp.arange(cluster_slots, dtype=jnp.int32)
    target_pick = (far_target[0][:, None] == slot_ids[None, :]).astype(jnp.float32)
    whole_table = lax.all_gather(send_slot, "clu", axis=0, tiled=True)
    own_index = lax.axis_index("clu")
    own_slots = lax.dynamic_slice_in_dim(whole_table, own_index * per_peer, per_peer, 1)
    source_pick = (own_slots[:, :, None] == slot_ids[None, None, :]).astype(jnp.float32)
    vector = start_vector * point_mask
    results = []
    for product in range(PRODUCTS):
        rounded = vector.astype(jnp.bfloat16)
        next_part = passed_along(rounded, "clu", -1)
        extended = jnp.concatenate([rounded, next_part], axis=0)
        source_vec = jnp.einsum(
            "qe,erb->qrb", second_bf, extended, preferred_element_type=jnp.float32
        ).astype(jnp.bfloat16)
        target_vec = jnp.einsum(
            "qe,erb->qrb", first_bf, extended, preferred_element_type=jnp.float32
        ).astype(jnp.bfloat16)
        forward = jnp.einsum(
            "qij,qrj->qri", near_blocks, source_vec, preferred_element_type=jnp.float32
        )
        backward = jnp.einsum(
            "qij,qri->qrj", near_blocks, target_vec, preferred_element_type=jnp.float32
        )
        near_sum = jnp.einsum("qe,qrb->erb", pick_first, forward, precision=highest)
        near_sum = near_sum + jnp.einsum("qe,qrb->erb", pick_second, backward, precision=highest)
        from_before = passed_along(near_sum[leaves:].astype(jnp.bfloat16), "clu", 1).astype(
            jnp.float32
        )
        output = jnp.einsum(
            "lij,lrj->lri", diag_blocks, rounded, preferred_element_type=jnp.float32
        )
        output = output + near_sum[:leaves] + from_before
        leaf_coef = jnp.einsum(
            "lkj,lrj->lrk", leaf_basis, rounded, preferred_element_type=jnp.float32
        )
        parent_coef = jnp.einsum("lrm,lmk->lrk", leaf_coef, transfer, precision=highest)
        parent_coef = parent_coef.reshape(leaves // 2, 2, rhs_count, rank).sum(axis=1)
        all_coef = jnp.concatenate([leaf_coef, parent_coef], axis=0).reshape(
            cluster_slots, coef_width
        )
        shard_rows = lax.all_gather(
            all_coef.reshape(1, cluster_slots * coef_width), "clu", axis=0, tiled=True
        )
        peers = shard_rows.shape[0]
        picked = jnp.einsum(
            "ncs,nsf->ncf",
            source_pick,
            shard_rows.reshape(peers, cluster_slots, coef_width),
            precision=highest,
        )
        source_coef = picked.reshape(peers * per_peer, coef_width)
        target_coef = jnp.dot(target_pick, all_coef, precision=highest).reshape(
            pair_rows, rhs_count, rank
        )
        far_in = jnp.einsum(
            "qkm,qrm->qrk",
            coupling,
            source_coef.reshape(pair_rows, rhs_count, rank),
            precision=highest,
        )
        far_out = jnp.einsum("qkm,qrk->qrm", coupling, target_coef, precision=highest).reshape(
            devices, per_peer, coef_width
        )
        local_far = jnp.dot(target_pick.T, far_in.reshape(pair_rows, coef_width), precision=highest)
        spread_peers = cluster_slots * lax.axis_size("clu") // cluster_slots
        placed = jnp.einsum("ncs,ncf->nsf", source_pick, far_out, precision=highest)
        returned = lax.psum_scatter(
            placed.reshape(spread_peers * cluster_slots, coef_width),
            "clu",
            scatter_dimension=0,
            tiled=True,
        )
        far_sum = (local_far + returned).reshape(cluster_slots, rhs_count, rank)
        parent_far = jnp.repeat(far_sum[leaves:], 2, axis=0)
        leaf_far = far_sum[:leaves] + jnp.einsum(
            "lmk,lrk->lrm", transfer, parent_far, precision=highest
        )
        leaf_round = leaf_far.astype(jnp.bfloat16)
        output = output + jnp.einsum(
            "lkj,lrk->lrj", leaf_basis, leaf_round, preferred_element_type=jnp.float32
        )
        vector = output * point_mask
        results.append(vector)
    return jnp.stack(results)


def solution(mesh):
    in_specs = (
        P("clu", None, None),
        P("clu"),
        P("clu", None, None),
        P("clu", None, None),
        P("clu"),
        P("clu"),
        P("clu"),
        P("clu", None, None),
        P("clu", None, None),
        P("clu", None, None),
        P("clu", None),
        P("clu", None),
    )
    out_specs = P(None, "clu", None, None)
    return jax.shard_map(
        on_device, mesh=mesh, in_specs=in_specs, out_specs=out_specs, check_vma=False
    )
```

profile of v0, /device:TPU:1, one launch (start us, length us, event | category | flops | bytes accessed | tf_op | source)
XLA Modules:
  0.0 2153.3 jit_solution(13738738667267111447)
XLA Ops:
  14.6 9.2 copy.123
  23.9 10.3 fusion.169
  35.8 38.7 %all-gather = s32[128,1,256]{2,1,0:T(1,128)S(1)} all-gather(s32[1,1,256]{2,1,0:T(1,128)S(1)} %bitcast.179), channel_id=1, replica_groups=mesh['clu'=128] {'clu'}, dimensions={0}, use_global_device_ids=true | all-gather | bytes 132096 | tf_op jit(solution)/shard_map/all_gather | solution.py:50
  80.2 323.9 %fusion = f32[8,512]{1,0:T(8,128)S(1)} fusion(f32[768,512]{1,0:T(8,128)} %reshape.136), kind=kCustom, calls=%all-reduce-scatter | all-reduce-scatter fusion | flops 524289 | bytes 1589248
  425.6 11.2 collective-permute-start.19
  438.9 13.5 collective-permute-start.21
  455.9 6.8 collective-permute-start.23
  498.3 45.3 %concatenate.32 = f32[262,512]{1,0:T(8,128)} concatenate(f32[6,512]{1,0:T(8,128)S(1)} %collective-permute-done.39, f32[8,512]{1,0:T(8,128)S(1)} %collective-permute-done.38, f32[8,512]{1,0:T(8,128)S(1)} %collective-permute-done.37, f32[8,512]{1,0:T(8,128)S(1)} %collective-permute-done.36, f32[8,512]{1,0:T(8,128)S(1)} %collective-permute-done.35, ...), dimensions={0} | concatenate | bytes 1073152
  555.5 16.4 fusion.168
  582.6 10.4 fusion.173
  600.1 329.2 %fusion.1 = f32[8,512]{1,0:T(8,128)S(1)} fusion(f32[768,512]{1,0:T(8,128)} %reshape.143), kind=kCustom, calls=%all-reduce-scatter.1 | all-reduce-scatter fusion | flops 524289 | bytes 1589248
  945.7 12.2 collective-permute-start.49
  962.5 8.0 collective-permute-start.52
  970.5 7.4 collective-permute-start.53
  981.1 7.8 collective-permute-start.55
  1019.7 45.3 %concatenate.33 = f32[262,512]{1,0:T(8,128)} concatenate(f32[6,512]{1,0:T(8,128)S(1)} %collective-permute-done.71, f32[8,512]{1,0:T(8,128)} %collective-permute-done.70, f32[8,512]{1,0:T(8,128)} %copy-done.22, f32[8,512]{1,0:T(8,128)S(1)} %collective-permute-done.68, f32[8,512]{1,0:T(8,128)S(1)} %collective-permute-done.67, f32[8,512]{1,0:T(8,128)S(1)} %collective-permute-done.66, ...), dimensions={0} | concatenate | bytes 1073152
  1077.0 16.4 fusion.172
  1104.0 10.4 fusion.177
  1121.5 329.8 %fusion.2 = f32[8,512]{1,0:T(8,128)S(1)} fusion(f32[768,512]{1,0:T(8,128)} %reshape.150), kind=kCustom, calls=%all-reduce-scatter.2 | all-reduce-scatter fusion | flops 524289 | bytes 1589248
  1459.4 7.6 collective-permute-start.73
  1476.4 15.0 collective-permute-start.79
  1494.3 6.5 collective-permute-start.82
  1546.1 45.3 %concatenate.34 = f32[262,512]{1,0:T(8,128)} concatenate(f32[6,512]{1,0:T(8,128)S(1)} %collective-permute-done.103, f32[8,512]{1,0:T(8,128)S(1)} %collective-permute-done.102, f32[8,512]{1,0:T(8,128)S(1)} %collective-permute-done.101, f32[8,512]{1,0:T(8,128)S(1)} %collective-permute-done.100, f32[8,512]{1,0:T(8,128)} %collective-permute-done.99, f32[8,512]{1,0:T(8,128)} %copy-done.23, ...), dimensions={0} | concatenate | bytes 1073152
  1603.4 16.4 fusion.176
  1630.2 10.4 fusion.181
  1647.7 329.6 %fusion.3 = f32[8,512]{1,0:T(8,128)S(1)} fusion(f32[768,512]{1,0:T(8,128)} %reshape.157), kind=kCustom, calls=%all-reduce-scatter.3 | all-reduce-scatter fusion | flops 524289 | bytes 1589248
  1993.7 12.1 collective-permute-start.113
  2010.5 8.0 collective-permute-start.116
  2018.5 7.4 collective-permute-start.117
  2029.1 7.7 collective-permute-start.119
  2067.5 45.3 %concatenate.35 = f32[262,512]{1,0:T(8,128)} concatenate(f32[6,512]{1,0:T(8,128)S(1)} %collective-permute-done.135, f32[8,512]{1,0:T(8,128)} %collective-permute-done.134, f32[8,512]{1,0:T(8,128)} %copy-done.24, f32[8,512]{1,0:T(8,128)S(1)} %collective-permute-done.132, f32[8,512]{1,0:T(8,128)S(1)} %collective-permute-done.131, f32[8,512]{1,0:T(8,128)S(1)} %collective-permute-done.130, ...), dimensions={0} | concatenate | bytes 1073152
  2125.7 16.2 fusion.180
  (467 shorter events, 357.3 us)
Async XLA Ops:
  6.5 537.3 %all-gather.10.cloned.1.call-start = ((), (), s32[]{:S(2)}) async-start(), calls=%async_computation | async-start | bytes 1585152 | tf_op jit(solution)/shard_map/all_gather | solution.py:89
  11.1 1054.2 %all-gather.12.cloned.1.call-start = ((), (), s32[]{:S(2)}) async-start(), calls=%async_computation.1 | async-start | bytes 1585152 | tf_op jit(solution)/shard_map/all_gather | solution.py:89
  420.3 32.1 %collective-permute-start.17 = (f32[8,512]{1,0:T(8,128)S(1)}, f32[8,512]{1,0:T(8,128)S(1)}, u32[]{:S(2)}, u32[]{:S(2)}) collective-permute-start(f32[8,512]{1,0:T(8,128)S(1)} %fusion), channel_id=1, source_target_pairs={{0,10},{1,11},{2,12},{3,13},{4,14},{5,15},{6,16},{7,17},{8,18},{9,... | collective-permute-start | bytes 49160
  424.2 31.7 %collective-permute-start.18 = (f32[8,512]{1,0:T(8,128)S(1)}, f32[8,512]{1,0:T(8,128)S(1)}, u32[]{:S(2)}, u32[]{:S(2)}) collective-permute-start(f32[8,512]{1,0:T(8,128)S(1)} %fusion), channel_id=1, source_target_pairs={{0,11},{1,12},{2,13},{3,14},{4,15},{5,16},{6,17},{7,18},{8,19},{9,... | collective-permute-start | bytes 49160
  425.6 37.2 %collective-permute-start.19 = (f32[8,512]{1,0:T(8,128)S(1)}, f32[8,512]{1,0:T(8,128)S(1)}, u32[]{:S(2)}, u32[]{:S(2)}) collective-permute-start(f32[8,512]{1,0:T(8,128)S(1)} %fusion), channel_id=1, source_target_pairs={{0,12},{1,13},{2,14},{3,15},{4,16},{5,17},{6,18},{7,19},{8,20},{9,... | collective-permute-start | bytes 49160
  436.8 28.8 %collective-permute-start.20 = (f32[8,512]{1,0:T(8,128)S(1)}, f32[8,512]{1,0:T(8,128)S(1)}, u32[]{:S(2)}, u32[]{:S(2)}) collective-permute-start(f32[8,512]{1,0:T(8,128)S(1)} %fusion), channel_id=1, source_target_pairs={{0,13},{1,14},{2,15},{3,16},{4,17},{5,18},{6,19},{7,20},{8,21},{9,... | collective-permute-start | bytes 49160
  438.9 29.6 %collective-permute-start.21 = (f32[8,512]{1,0:T(8,128)S(1)}, f32[8,512]{1,0:T(8,128)S(1)}, u32[]{:S(2)}, u32[]{:S(2)}) collective-permute-start(f32[8,512]{1,0:T(8,128)S(1)} %fusion), channel_id=1, source_target_pairs={{0,14},{1,15},{2,16},{3,17},{4,18},{5,19},{6,20},{7,21},{8,22},{9,... | collective-permute-start | bytes 49160
  497.9 78.5 %collective-permute-start.1 = (bf16[4,8,256]{2,1,0:T(8,128)(2,1)}, bf16[4,8,256]{2,1,0:T(8,128)(2,1)}, u32[]{:S(2)}, u32[]{:S(2)}) collective-permute-start(bf16[4,8,256]{2,1,0:T(8,128)(2,1)} %slice.131), channel_id=1, source_target_pairs={{0,1},{1,2},{2,3},{3,4},{4,5},{5,6},{6,7},{7,8},{8,9},{9,10},{10,1... | collective-permute-start | bytes 49160 | tf_op jit(solution)/shard_map/ppermute | solution.py:12
  577.9 357.3 %collective-permute-start.2 = (bf16[4,8,256]{2,1,0:T(8,128)(2,1)S(1)}, bf16[4,8,256]{2,1,0:T(8,128)(2,1)S(1)}, u32[]{:S(2)}, u32[]{:S(2)}) collective-permute-start(bf16[4,8,256]{2,1,0:T(8,128)(2,1)S(1)} %get-tuple-element.5), channel_id=1, source_target_pairs={{0,127},{1,0},{2,1},{3,2},{4,3},{5,4},{6,5},{7,6},{8,7},{9,8},{10,... | collective-permute-start | bytes 49160 | tf_op jit(solution)/shard_map/ppermute | solution.py:12
  579.8 1011.8 %all-gather.14.cloned.1.call-start = ((), (), s32[]{:S(2)}) async-start(), calls=%async_computation.2 | async-start | bytes 1585152 | tf_op jit(solution)/shard_map/all_gather | solution.py:89
  941.9 20.6 collective-permute-start.47
  943.2 27.3 %collective-permute-start.48 = (f32[8,512]{1,0:T(8,128)S(1)}, f32[8,512]{1,0:T(8,128)S(1)}, u32[]{:S(2)}, u32[]{:S(2)}) collective-permute-start(f32[8,512]{1,0:T(8,128)S(1)} %fusion.1), channel_id=1, source_target_pairs={{0,9},{1,10},{2,11},{3,12},{4,13},{5,14},{6,15},{7,16},{8,17},{9,1... | collective-permute-start | bytes 49160
  945.7 32.2 %collective-permute-start.49 = (f32[8,512]{1,0:T(8,128)S(1)}, f32[8,512]{1,0:T(8,128)S(1)}, u32[]{:S(2)}, u32[]{:S(2)}) collective-permute-start(f32[8,512]{1,0:T(8,128)S(1)} %fusion.1), channel_id=1, source_target_pairs={{0,10},{1,11},{2,12},{3,13},{4,14},{5,15},{6,16},{7,17},{8,18},{9,... | collective-permute-start | bytes 49160
  957.9 23.2 %collective-permute-start.50 = (f32[8,512]{1,0:T(8,128)S(1)}, f32[8,512]{1,0:T(8,128)S(1)}, u32[]{:S(2)}, u32[]{:S(2)}) collective-permute-start(f32[8,512]{1,0:T(8,128)S(1)} %fusion.1), channel_id=1, source_target_pairs={{0,11},{1,12},{2,13},{3,14},{4,15},{5,16},{6,17},{7,18},{8,19},{9,... | collective-permute-start | bytes 49160
  960.9 28.3 %collective-permute-start.51 = (f32[8,512]{1,0:T(8,128)S(1)}, f32[8,512]{1,0:T(8,128)S(1)}, u32[]{:S(2)}, u32[]{:S(2)}) collective-permute-start(f32[8,512]{1,0:T(8,128)S(1)} %fusion.1), channel_id=1, source_target_pairs={{0,12},{1,13},{2,14},{3,15},{4,16},{5,17},{6,18},{7,19},{8,20},{9,... | collective-permute-start | bytes 49160
  962.5 28.6 %collective-permute-start.52 = (f32[8,512]{1,0:T(8,128)S(1)}, f32[8,512]{1,0:T(8,128)S(1)}, u32[]{:S(2)}, u32[]{:S(2)}) collective-permute-start(f32[8,512]{1,0:T(8,128)S(1)} %fusion.1), channel_id=1, source_target_pairs={{0,13},{1,14},{2,15},{3,16},{4,17},{5,18},{6,19},{7,20},{8,21},{9,... | collective-permute-start | bytes 49160
  970.5 22.3 %collective-permute-start.53 = (f32[8,512]{1,0:T(8,128)S(1)}, f32[8,512]{1,0:T(8,128)S(1)}, u32[]{:S(2)}, u32[]{:S(2)}) collective-permute-start(f32[8,512]{1,0:T(8,128)S(1)} %fusion.1), channel_id=1, source_target_pairs={{0,14},{1,15},{2,16},{3,17},{4,18},{5,19},{6,20},{7,21},{8,22},{9,... | collective-permute-start | bytes 49160
  1018.5 79.3 %collective-permute-start.3 = (bf16[4,8,256]{2,1,0:T(8,128)(2,1)}, bf16[4,8,256]{2,1,0:T(8,128)(2,1)}, u32[]{:S(2)}, u32[]{:S(2)}) collective-permute-start(bf16[4,8,256]{2,1,0:T(8,128)(2,1)} %slice.130), channel_id=1, source_target_pairs={{0,1},{1,2},{2,3},{3,4},{4,5},{5,6},{6,7},{7,8},{8,9},{9,10},{10,1... | collective-permute-start | bytes 49160 | tf_op jit(solution)/shard_map/ppermute | solution.py:12
  1099.3 357.9 %collective-permute-start.4 = (bf16[4,8,256]{2,1,0:T(8,128)(2,1)S(1)}, bf16[4,8,256]{2,1,0:T(8,128)(2,1)S(1)}, u32[]{:S(2)}, u32[]{:S(2)}) collective-permute-start(bf16[4,8,256]{2,1,0:T(8,128)(2,1)S(1)} %get-tuple-element.7), channel_id=1, source_target_pairs={{0,127},{1,0},{2,1},{3,2},{4,3},{5,4},{6,5},{7,6},{8,7},{9,8},{10,... | collective-permute-start | bytes 49160 | tf_op jit(solution)/shard_map/ppermute | solution.py:12
  1101.3 1011.8 %all-gather.16.cloned.1.call-start = ((), (), s32[]{:S(2)}) async-start(), calls=%async_computation.3 | async-start | bytes 1585152 | tf_op jit(solution)/shard_map/all_gather | solution.py:89
  1475.1 25.7 %collective-permute-start.78 = (f32[8,512]{1,0:T(8,128)S(1)}, f32[8,512]{1,0:T(8,128)S(1)}, u32[]{:S(2)}, u32[]{:S(2)}) collective-permute-start(f32[8,512]{1,0:T(8,128)S(1)} %fusion.2), channel_id=1, source_target_pairs={{0,7},{1,8},{2,9},{3,10},{4,11},{5,12},{6,13},{7,14},{8,15},{9,16}... | collective-permute-start | bytes 49160
  1476.4 28.3 %collective-permute-start.79 = (f32[8,512]{1,0:T(8,128)S(1)}, f32[8,512]{1,0:T(8,128)S(1)}, u32[]{:S(2)}, u32[]{:S(2)}) collective-permute-start(f32[8,512]{1,0:T(8,128)S(1)} %fusion.2), channel_id=1, source_target_pairs={{0,8},{1,9},{2,10},{3,11},{4,12},{5,13},{6,14},{7,15},{8,16},{9,17... | collective-permute-start | bytes 49160
  1494.3 22.4 %collective-permute-start.82 = (f32[8,512]{1,0:T(8,128)S(1)}, f32[8,512]{1,0:T(8,128)S(1)}, u32[]{:S(2)}, u32[]{:S(2)}) collective-permute-start(f32[8,512]{1,0:T(8,128)S(1)} %fusion.2), channel_id=1, source_target_pairs={{0,11},{1,12},{2,13},{3,14},{4,15},{5,16},{6,17},{7,18},{8,19},{9,... | collective-permute-start | bytes 49160
  1545.1 79.1 %collective-permute-start.5 = (bf16[4,8,256]{2,1,0:T(8,128)(2,1)}, bf16[4,8,256]{2,1,0:T(8,128)(2,1)}, u32[]{:S(2)}, u32[]{:S(2)}) collective-permute-start(bf16[4,8,256]{2,1,0:T(8,128)(2,1)} %slice.129), channel_id=1, source_target_pairs={{0,1},{1,2},{2,3},{3,4},{4,5},{5,6},{6,7},{7,8},{8,9},{9,10},{10,1... | collective-permute-start | bytes 49160 | tf_op jit(solution)/shard_map/ppermute | solution.py:12
  1626.8 356.4 %collective-permute-start.6 = (bf16[4,8,256]{2,1,0:T(8,128)(2,1)S(1)}, bf16[4,8,256]{2,1,0:T(8,128)(2,1)S(1)}, u32[]{:S(2)}, u32[]{:S(2)}) collective-permute-start(bf16[4,8,256]{2,1,0:T(8,128)(2,1)S(1)} %get-tuple-element.9), channel_id=1, source_target_pairs={{0,127},{1,0},{2,1},{3,2},{4,3},{5,4},{6,5},{7,6},{8,7},{9,8},{10,... | collective-permute-start | bytes 49160 | tf_op jit(solution)/shard_map/ppermute | solution.py:12
  1991.2 27.3 %collective-permute-start.112 = (f32[8,512]{1,0:T(8,128)S(1)}, f32[8,512]{1,0:T(8,128)S(1)}, u32[]{:S(2)}, u32[]{:S(2)}) collective-permute-start(f32[8,512]{1,0:T(8,128)S(1)} %fusion.3), channel_id=1, source_target_pairs={{0,9},{1,10},{2,11},{3,12},{4,13},{5,14},{6,15},{7,16},{8,17},{9,1... | collective-permute-start | bytes 49160
  1993.7 32.1 %collective-permute-start.113 = (f32[8,512]{1,0:T(8,128)S(1)}, f32[8,512]{1,0:T(8,128)S(1)}, u32[]{:S(2)}, u32[]{:S(2)}) collective-permute-start(f32[8,512]{1,0:T(8,128)S(1)} %fusion.3), channel_id=1, source_target_pairs={{0,10},{1,11},{2,12},{3,13},{4,14},{5,15},{6,16},{7,17},{8,18},{9,... | collective-permute-start | bytes 49160
  2005.8 23.3 %collective-permute-start.114 = (f32[8,512]{1,0:T(8,128)S(1)}, f32[8,512]{1,0:T(8,128)S(1)}, u32[]{:S(2)}, u32[]{:S(2)}) collective-permute-start(f32[8,512]{1,0:T(8,128)S(1)} %fusion.3), channel_id=1, source_target_pairs={{0,11},{1,12},{2,13},{3,14},{4,15},{5,16},{6,17},{7,18},{8,19},{9,... | collective-permute-start | bytes 49160
  2008.9 28.3 %collective-permute-start.115 = (f32[8,512]{1,0:T(8,128)S(1)}, f32[8,512]{1,0:T(8,128)S(1)}, u32[]{:S(2)}, u32[]{:S(2)}) collective-permute-start(f32[8,512]{1,0:T(8,128)S(1)} %fusion.3), channel_id=1, source_target_pairs={{0,12},{1,13},{2,14},{3,15},{4,16},{5,17},{6,18},{7,19},{8,20},{9,... | collective-permute-start | bytes 49160
  2010.5 28.6 %collective-permute-start.116 = (f32[8,512]{1,0:T(8,128)S(1)}, f32[8,512]{1,0:T(8,128)S(1)}, u32[]{:S(2)}, u32[]{:S(2)}) collective-permute-start(f32[8,512]{1,0:T(8,128)S(1)} %fusion.3), channel_id=1, source_target_pairs={{0,13},{1,14},{2,15},{3,16},{4,17},{5,18},{6,19},{7,20},{8,21},{9,... | collective-permute-start | bytes 49160
  2018.5 22.3 %collective-permute-start.117 = (f32[8,512]{1,0:T(8,128)S(1)}, f32[8,512]{1,0:T(8,128)S(1)}, u32[]{:S(2)}, u32[]{:S(2)}) collective-permute-start(f32[8,512]{1,0:T(8,128)S(1)} %fusion.3), channel_id=1, source_target_pairs={{0,14},{1,15},{2,16},{3,17},{4,18},{5,19},{6,20},{7,21},{8,22},{9,... | collective-permute-start | bytes 49160
  2066.5 78.6 %collective-permute-start.7 = (bf16[4,8,256]{2,1,0:T(8,128)(2,1)}, bf16[4,8,256]{2,1,0:T(8,128)(2,1)}, u32[]{:S(2)}, u32[]{:S(2)}) collective-permute-start(bf16[4,8,256]{2,1,0:T(8,128)(2,1)} %slice.128), channel_id=1, source_target_pairs={{0,1},{1,2},{2,3},{3,4},{4,5},{5,6},{6,7},{7,8},{8,9},{9,10},{10,1... | collective-permute-start | bytes 49160 | tf_op jit(solution)/shard_map/ppermute | solution.py:12
  (134 other events, 4648.2 us)
Sparse Core Ops, SparseCore 0:
  11.2 67.8 all-gather.9
  579.9 63.7 all-gather.11
  1101.4 64.4 all-gather.13
  1627.8 64.4 all-gather.15
where the time goes:
time: 2190 us; the launch traced here: 2150 us
  blocking collectives  1350 us (62%)
  starting transfers between devices  355 us (16%)
  local copies, waits for them, and re-layouts  267 us (12%)
  matrix products  158 us (7%)
    unnamed x4, blocking collectives  1310 us
    unnamed x128, starting transfers between devices  346 us
    unnamed x65, local copies, waits for them, and re-layouts  197 us
    dot_general x4, matrix products, on_device(): jnp.einsum('qkm,qrm->qrk', coupling, source_coef.reshape(pair_rows, rhs_c...  65.3 us
  transfers between devices with their start and end apart: 140, of which 5 were waited for; matrix products, arithmetic and copies ran while one was open for 80% of the time, Pallas kernels for 0%

commit v1 on v0

v1 whole, which is shorter than its diff:
```python
import functools

import jax
import jax.numpy as jnp
from jax import lax
from jax.experimental import pallas as pl
from jax.experimental.pallas import tpu as pltpu
from jax.sharding import PartitionSpec as P

PRODUCTS = 4
REACH = 8
NEAR = 2 * REACH + 1
GROUPS = 3
LOADS = 4
LEAVES = 4
RANK = 64
RHS = 8
POINTS = 256
CAPACITY = 16
MESH = pl.DeviceIdType.MESH
F32 = jnp.float32
BF16 = jnp.bfloat16


def nn(a, b):
    return jnp.dot(a, b, preferred_element_type=F32)


def nt(a, b):
    return lax.dot_general(a, b, (((1,), (1,)), ((), ())), preferred_element_type=F32)


def swap_halves(a):
    return pltpu.roll(a, RANK, 1)


def pairs_of(first, last):
    return [list(range(j, min(j + 2, last))) for j in range(first, last, 2)]


def side_by_side(parts):
    return parts[0] if len(parts) == 1 else jnp.concatenate(parts, axis=1)


def kernel(
    devices,
    start,
    leaf_size,
    diag_hbm,
    near_hbm,
    near_count,
    near_first,
    near_second,
    basis,
    transfer,
    coupling,
    send_slot,
    far_target,
    out,
    parent_raw,
    leaf_raw,
    parent_w,
    leaf_w,
    near,
    diag,
    both_basis,
    pick,
    point_mask,
    vector,
    extended,
    send,
    recv,
    x_out,
    x_in,
    near_out,
    near_in,
    load_sem,
    send_sem,
    recv_sem,
    side_sem,
):
    me = lax.axis_index("clu")
    far_count = devices - NEAR
    group = far_count // GROUPS
    load_rows = devices // LOADS

    def peer(j):
        return lax.rem(me + (j - REACH + devices), devices)

    def tile_of(j):
        return 2 * j if j < NEAR else j + NEAR

    parent_loads = [
        pltpu.make_async_copy(
            coupling.at[pl.ds(c * load_rows, load_rows), 1],
            parent_raw.at[pl.ds(c * load_rows, load_rows)],
            load_sem.at[c],
        )
        for c in range(LOADS)
    ]
    near_load = pltpu.make_async_copy(near_hbm, near, load_sem.at[LOADS + 1])
    diag_load = pltpu.make_async_copy(diag_hbm, diag, load_sem.at[LOADS + 2])
    for j in range(NEAR):
        pltpu.make_async_copy(
            coupling.at[peer(j), 0], leaf_raw.at[j], load_sem.at[LOADS]
        ).start()
    for load in parent_loads:
        load.start()
    near_load.start()
    diag_load.start()

    barrier = pltpu.get_barrier_semaphore()

    def greet(step, carry):
        pl.semaphore_signal(
            barrier, inc=1, device_id=(lax.rem(me + step, devices),), device_id_type=MESH
        )
        return carry

    lax.fori_loop(1, devices, greet, 0)

    point_ids = lax.broadcasted_iota(jnp.int32, (RHS, POINTS), 1)
    for l in range(LEAVES):
        inside = jnp.where(point_ids < leaf_size[l], 1.0, 0.0)
        point_mask[l] = inside
        vector[l] = start[l] * inside
    for e in range(CAPACITY):
        live = e < near_count[0]
        for t in range(LEAVES):
            pick[e, t] = jnp.where(live & (near_first[e] == t), 1.0, 0.0)
        for s in range(2 * LEAVES):
            pick[e, LEAVES + s] = jnp.where(live & (near_second[e] == s), 1.0, 0.0)

    for l in range(LEAVES):
        moved = transfer[l].T
        high = moved.astype(BF16)
        low = (moved - high.astype(F32)).astype(BF16)
        own = basis[l]
        both_basis[l] = jnp.concatenate(
            [own.astype(F32), nn(high, own) + nn(low, own)], axis=0
        ).astype(BF16)

    lane = lax.broadcasted_iota(jnp.int32, (RANK, 2 * RANK), 1)
    row = lax.broadcasted_iota(jnp.int32, (RANK, 2 * RANK), 0)
    unit = jnp.where(lane == row + RANK, 1.0, 0.0)
    left = lane < RANK

    def weights(raw, target, source, slots):
        wide = jnp.where(left, jnp.concatenate([raw, raw], axis=1), unit)
        slot = jnp.where(left, target, source)
        return [jnp.where(slot == s, wide, 0.0).astype(BF16) for s in slots]

    pltpu.make_async_copy(leaf_raw, leaf_raw, load_sem.at[LOADS]).wait()

    def build_leaf(j, carry):
        column = 2 * peer(j)
        parts = weights(
            leaf_raw[j], far_target[0, column], send_slot[0, column], range(LEAVES)
        )
        for s, part in enumerate(parts):
            leaf_w[j, s * RANK : (s + 1) * RANK, :] = part
        return carry

    lax.fori_loop(0, NEAR, build_leaf, 0)

    def build_parent(p, carry):
        column = 2 * p + 1
        parts = weights(
            parent_raw[p],
            far_target[0, column],
            send_slot[0, column],
            range(LEAVES, LEAVES + LEAVES // 2),
        )
        j = lax.rem(p - me + (REACH + devices), devices)
        for s, part in enumerate(parts):
            parent_w[j, s * RANK : (s + 1) * RANK, :] = part
        return carry

    for c in range(LOADS):
        parent_loads[c].wait()
        lax.fori_loop(c * load_rows, (c + 1) * load_rows, build_parent, 0)

    near_load.wait()
    diag_load.wait()
    pl.semaphore_wait(barrier, devices - 1)

    half = lax.broadcasted_iota(jnp.int32, (RHS, 2 * RANK), 1) < RANK

    def remote(src, dst, out_sem, in_sem, target):
        return pltpu.make_async_remote_copy(
            src_ref=src,
            dst_ref=dst,
            send_sem=out_sem,
            recv_sem=in_sem,
            device_id=(target,),
            device_id_type=MESH,
        )

    def x_copy(n):
        return remote(
            x_out.at[n], x_in.at[n], side_sem.at[n, 0], side_sem.at[n, 1], peer(REACH - 1)
        )

    def near_copy(n):
        return remote(
            near_out.at[n], near_in.at[n], side_sem.at[n, 2], side_sem.at[n, 3], peer(REACH + 1)
        )

    def far_copy(n, j):
        if j < NEAR:
            src, dst, count, box = tile_of(j), tile_of(NEAR - 1 - j), 2, 0
        else:
            src, dst, count = tile_of(j), tile_of(devices + NEAR - 1 - j), 1
            box = 1 + (j - NEAR) // group
        return remote(
            send.at[n, pl.ds(src, count)],
            recv.at[n, pl.ds(dst, count)],
            send_sem.at[n],
            recv_sem.at[n, box],
            peer(j),
        )

    def product(n, carry):
        exact = [vector[l] for l in range(LEAVES)]
        rounded = [value.astype(BF16) for value in exact]
        x_out[n] = jnp.concatenate(exact, axis=0).astype(BF16)
        x_copy(n).start()

        coef = [nt(rounded[l], both_basis[l]) for l in range(LEAVES)]
        leaf_coef = jnp.concatenate(
            [
                jnp.where(half, coef[0], swap_halves(coef[1])),
                jnp.where(half, coef[2], swap_halves(coef[3])),
            ],
            axis=1,
        ).astype(BF16)
        parent_coef = jnp.where(
            half, swap_halves(coef[0] + coef[1]), coef[2] + coef[3]
        ).astype(BF16)

        def fill(values, w, first, last, place):
            for js in pairs_of(first, last):
                made = nn(values, side_by_side([w[j] for j in js]))
                for i, j in enumerate(js):
                    tile = swap_halves(made[:, i * 2 * RANK : (i + 1) * 2 * RANK]).astype(BF16)
                    if j == REACH:
                        recv[n, place(j)] = tile
                    else:
                        send[n, place(j)] = tile

        fill(leaf_coef, leaf_w, 0, NEAR, lambda j: tile_of(j) + 1)
        fill(parent_coef, parent_w, 0, NEAR, tile_of)
        for j in range(NEAR):
            if j != REACH:
                far_copy(n, j).start()
        for g in range(GROUPS):
            first = NEAR + g * group
            fill(parent_coef, parent_w, first, first + group, tile_of)
            for j in range(first, first + group):
                far_copy(n, j).start()

        for l in range(LEAVES):
            extended[l] = rounded[l].astype(F32)
        backward = jnp.zeros((2 * LEAVES * RHS, POINTS), F32)
        for e in range(CAPACITY):
            own = extended[near_first[e]]
            spread = jnp.concatenate(
                [own * pick[e, LEAVES + s] for s in range(2 * LEAVES)], axis=0
            ).astype(BF16)
            backward = backward + nn(spread, near[e])
        near_out[n] = backward[LEAVES * RHS :].astype(BF16)
        near_copy(n).start()
        total = backward[: LEAVES * RHS] + jnp.concatenate(
            [nn(rounded[l], diag[l]) for l in range(LEAVES)], axis=0
        )

        x_copy(n).wait_recv()
        following = x_in[n].astype(F32)
        for l in range(LEAVES):
            extended[LEAVES + l] = following[l * RHS : (l + 1) * RHS]
        for e in range(CAPACITY):
            other = extended[near_second[e]]
            spread = jnp.concatenate(
                [other * pick[e, t] for t in range(LEAVES)], axis=0
            ).astype(BF16)
            total = total + nt(spread, near[e])

        def take(w, first, last, place, sofar):
            for js in pairs_of(first, last):
                got = side_by_side([recv[n, place(j)] for j in js])
                sofar = sofar + nt(got, side_by_side([w[j] for j in js]))
            return sofar

        def arrived(first, count, box):
            tiles = recv.at[n, pl.ds(first, count)]
            pltpu.make_async_copy(tiles, tiles, recv_sem.at[n, box]).wait()

        arrived(0, 2 * (NEAR - 1), 0)
        leaf_far = jnp.zeros((RHS, LEAVES * RANK), F32)
        leaf_far = take(leaf_w, 0, NEAR, lambda j: tile_of(j) + 1, leaf_far)
        parent_far = jnp.zeros((RHS, 2 * RANK), F32)
        parent_far = take(parent_w, 0, NEAR, tile_of, parent_far)
        for g in range(GROUPS):
            first = devices - (g + 1) * group
            arrived(tile_of(first), group, 1 + g)
            parent_far = take(parent_w, first, first + group, tile_of, parent_far)

        near_copy(n).wait_recv()
        total = total + near_in[n].astype(F32)
        for l in range(LEAVES):
            pair = leaf_far[:, (l // 2) * 2 * RANK : (l // 2 + 1) * 2 * RANK]
            both = jnp.where(
                half,
                pair if l % 2 == 0 else swap_halves(pair),
                swap_halves(parent_far) if l < 2 else parent_far,
            ).astype(BF16)
            value = total[l * RHS : (l + 1) * RHS] + nn(both, both_basis[l])
            value = value * point_mask[l]
            vector[l] = value
            out[n, l] = value
        return carry

    lax.fori_loop(0, PRODUCTS, product, 0)

    def finish(n, carry):
        sent = send.at[n, pl.ds(0, 2 * (NEAR - 1) + far_count)]
        pltpu.make_async_copy(sent, sent, send_sem.at[n]).wait()
        x_copy(n).wait_send()
        near_copy(n).wait_send()
        return carry

    lax.fori_loop(0, PRODUCTS, finish, 0)


def on_device(
    start_vector,
    leaf_size,
    diag_blocks,
    near_blocks,
    near_count,
    near_first,
    near_second,
    leaf_basis,
    transfer,
    coupling,
    send_slot,
    far_target,
):
    devices = lax.axis_size("clu")
    tiles = devices + NEAR
    vmem = pl.BlockSpec(memory_space=pltpu.VMEM)
    smem = pl.BlockSpec(memory_space=pltpu.SMEM)
    anywhere = pl.BlockSpec(memory_space=pl.ANY)
    sides = (PRODUCTS, LEAVES * RHS, POINTS)
    return pl.pallas_call(
        functools.partial(kernel, devices),
        out_shape=jax.ShapeDtypeStruct((PRODUCTS, LEAVES, RHS, POINTS), F32),
        in_specs=[
            vmem,
            smem,
            anywhere,
            anywhere,
            smem,
            smem,
            smem,
            vmem,
            vmem,
            anywhere,
            smem,
            smem,
        ],
        out_specs=vmem,
        scratch_shapes=[
            pltpu.VMEM((devices, RANK, RANK), F32),
            pltpu.VMEM((NEAR, RANK, RANK), F32),
            pltpu.VMEM((devices, 2 * RANK, 2 * RANK), BF16),
            pltpu.VMEM((NEAR, LEAVES * RANK, 2 * RANK), BF16),
            pltpu.VMEM((CAPACITY, POINTS, POINTS), BF16),
            pltpu.VMEM((LEAVES, POINTS, POINTS), BF16),
            pltpu.VMEM((LEAVES, 2 * RANK, POINTS), BF16),
            pltpu.SMEM((CAPACITY, 3 * LEAVES), F32),
            pltpu.VMEM((LEAVES, RHS, POINTS), F32),
            pltpu.VMEM((LEAVES, RHS, POINTS), F32),
            pltpu.VMEM((2 * LEAVES, RHS, POINTS), F32),
            pltpu.VMEM((PRODUCTS, tiles, RHS, 2 * RANK), BF16),
            pltpu.VMEM((PRODUCTS, tiles, RHS, 2 * RANK), BF16),
            pltpu.VMEM(sides, BF16),
            pltpu.VMEM(sides, BF16),
            pltpu.VMEM(sides, BF16),
            pltpu.VMEM(sides, BF16),
            pltpu.SemaphoreType.DMA((LOADS + 3,)),
            pltpu.SemaphoreType.DMA((PRODUCTS,)),
            pltpu.SemaphoreType.DMA((PRODUCTS, 1 + GROUPS)),
            pltpu.SemaphoreType.DMA((PRODUCTS, 4)),
        ],
        compiler_params=pltpu.CompilerParams(
            collective_id=0, has_side_effects=True, vmem_limit_bytes=48 * 1024 * 1024
        ),
        name="h2_products",
    )(
        start_vector,
        leaf_size,
        diag_blocks,
        near_blocks,
        near_count,
        near_first,
        near_second,
        leaf_basis,
        transfer,
        coupling.reshape(devices, 2, RANK, RANK),
        send_slot,
        far_target,
    )


def solution(mesh):
    in_specs = (
        P("clu", None, None),
        P("clu"),
        P("clu", None, None),
        P("clu", None, None),
        P("clu"),
        P("clu"),
        P("clu"),
        P("clu", None, None),
        P("clu", None, None),
        P("clu", None, None),
        P("clu", None),
        P("clu", None),
    )
    out_specs = P(None, "clu", None, None)
    return jax.shard_map(
        on_device, mesh=mesh, in_specs=in_specs, out_specs=out_specs, check_vma=False
    )
```

time: 2190 us -> 71.4 us (0.03); the launches traced: 2150 us -> 71.2 us
  blocking collectives: 1350 us -> 0 us
  starting transfers between devices: 355 us -> 0 us
  local copies, waits for them, and re-layouts: 267 us -> 10 us
  matrix products: 158 us -> 0 us
  Pallas kernels: 0 us -> 60.4 us
    unnamed x4 -> x0, blocking collectives: 1310 us -> none
    unnamed x128 -> x0, starting transfers between devices: 346 us -> none
    unnamed x65 -> x22, local copies, waits for them, and re-layouts: 197 us -> 10 us
    dot_general x68 -> x0, matrix products: 158 us -> none  [the longest x4 65.3 us: on_device(): jnp.einsum('qkm,qrm->qrk', coupling, source_coef.reshape(pair_rows, rhs_c...]
    pallas_call x0 -> x1, Pallas kernels: none -> 60.4 us  [on_device(): pl.pallas_call(functools.partial(kernel, devices), out_shape=jax.ShapeDty...]
    all_gather x1 -> x0, blocking collectives: 38.7 us -> none  [on_device(): whole_table = lax.all_gather(send_slot, 'clu', axis=0, tiled=True)]
    reshape x16 -> x0, local copies, waits for them, and re-layouts: 29.1 us -> none  [the longest x4 11.8 us: on_device(): shard_rows.reshape(peers, cluster_slots, coef_width)]
  transfers between devices with their start and end apart: 140 -> 0, of which waited for: 5 -> 0; matrix products, arithmetic and copies ran while one was open for 80% -> 0% of each run, Pallas kernels for 0% -> 0%
where the time goes in v1:
time: 71.4 us; the launch traced here: 71.2 us
  Pallas kernels  60.4 us (85%)
  local copies, waits for them, and re-layouts  10 us (14%)
  between operations  0.8 us (1%)
    pallas_call x1, Pallas kernels, on_device(): pl.pallas_call(functools.partial(kernel, devices), out_shape=jax.ShapeDty...  60.4 us
    unnamed x22, local copies, waits for them, and re-layouts  10 us

profile of v1, /device:TPU:1, one launch (start us, length us, event | category | flops | bytes accessed | tf_op | source)
XLA Modules:
  0.0 71.2 jit_solution(14085291130022954497)
XLA Ops:
  0.7 0.0 copy-start
  0.7 0.0 copy-start.1
  0.7 0.0 copy-start.2
  0.7 0.0 copy-start.3
  0.7 0.0 copy-start.4
  0.7 0.0 copy-start.5
  0.7 0.0 copy-start.6
  0.7 0.0 copy-start.7
  0.7 0.0 copy-start.8
  0.7 0.0 copy-start.9
  0.8 9.3 %copy.13 = f32[256,64,64]{2,1,0:T(8,128)} copy(f32[256,64,64]{0,2,1:T(8,128)} %param.21) | data formatting | bytes 8388608 | tf_op args[9]
  10.1 0.0 copy-done
  10.1 0.0 copy-done.1
  10.1 0.0 copy-done.2
  10.1 0.0 copy-done.3
  10.1 0.0 copy-done.4
  10.1 0.0 copy-done.5
  10.1 0.0 copy-done.6
  10.1 0.0 copy-done.7
  10.1 0.0 copy-done.8
  10.1 0.0 copy-done.9
  10.1 60.4 %h2_products.1 = f32[4,4,8,256]{3,2,1,0:T(8,128)S(1)} custom-call(f32[4,8,256]{2,1,0:T(8,128)S(1)} %copy-done.4, s32[4]{0:T(128)S(1)} %copy-done.7, bf16[4,256,256]{2,1,0:T(8,128)(2,1)S(1)} %copy-done.1, bf16[16,256,256]{2,1,0:T(8,128)(2,1)S(1)} %copy-done, s32[1]{0:T(128)S(6)} %copy.15.near_count, s32[16]{0:T(128)S(1)} %copy-done.8, s32[16]{0:T(128)S(1)} %copy-done.9, ...), custom_call_target="tpu_custom_call" | custom-call | tf_op jit(solution)/shard_map/h2_products/pallas_call | solution.py:355
  70.6 0.7 copy.16
Async XLA Ops:
  0.7 9.4 %copy-start = (bf16[16,256,256]{2,1,0:T(8,128)(2,1)S(1)}, bf16[16,256,256]{2,1,0:T(8,128)(2,1)}, u32[]{:S(2)}) copy-start(bf16[16,256,256]{2,1,0:T(8,128)(2,1)} %near_hbm.1) | copy-start | bytes 6291460
  0.7 9.4 %copy-start.1 = (bf16[4,256,256]{2,1,0:T(8,128)(2,1)S(1)}, bf16[4,256,256]{2,1,0:T(8,128)(2,1)}, u32[]{:S(2)}) copy-start(bf16[4,256,256]{2,1,0:T(8,128)(2,1)} %diag_hbm.1) | copy-start | bytes 1572868
  0.7 9.4 %copy-start.2 = (bf16[4,64,256]{2,1,0:T(8,128)(2,1)S(1)}, bf16[4,64,256]{2,1,0:T(8,128)(2,1)}, u32[]{:S(2)}) copy-start(bf16[4,64,256]{2,1,0:T(8,128)(2,1)} %basis.1) | copy-start | bytes 393220
  0.7 9.4 %copy-start.3 = (f32[4,64,64]{2,1,0:T(8,128)S(1)}, f32[4,64,64]{2,1,0:T(8,128)}, u32[]{:S(2)}) copy-start(f32[4,64,64]{2,1,0:T(8,128)} %transfer.1) | copy-start | bytes 196612
  0.7 9.4 %copy-start.4 = (f32[4,8,256]{2,1,0:T(8,128)S(1)}, f32[4,8,256]{2,1,0:T(8,128)}, u32[]{:S(2)}) copy-start(f32[4,8,256]{2,1,0:T(8,128)} %start.1) | copy-start | bytes 98308
  0.7 9.4 %copy-start.5 = (s32[1,256]{1,0:T(1,128)S(1)}, s32[1,256]{1,0:T(1,128)}, u32[]{:S(2)}) copy-start(s32[1,256]{1,0:T(1,128)} %send_slot.1) | copy-start | bytes 3076
  0.7 9.4 %copy-start.6 = (s32[1,256]{1,0:T(1,128)S(1)}, s32[1,256]{1,0:T(1,128)}, u32[]{:S(2)}) copy-start(s32[1,256]{1,0:T(1,128)} %far_target.1) | copy-start | bytes 3076
  0.7 9.4 %copy-start.7 = (s32[4]{0:T(128)S(1)}, s32[4]{0:T(128)}, u32[]{:S(2)}) copy-start(s32[4]{0:T(128)} %leaf_size.1) | copy-start | bytes 52
  0.7 9.4 %copy-start.8 = (s32[16]{0:T(128)S(1)}, s32[16]{0:T(128)}, u32[]{:S(2)}) copy-start(s32[16]{0:T(128)} %near_first.1) | copy-start | bytes 196
  0.7 9.4 %copy-start.9 = (s32[16]{0:T(128)S(1)}, s32[16]{0:T(128)}, u32[]{:S(2)}) copy-start(s32[16]{0:T(128)} %near_second.1) | copy-start | bytes 196

commit v2 on v1

--- a/solution.py
+++ b/solution.py
@@ -14,6 +14,7 @@
 LOADS = 4
 LEAVES = 4
 RANK = 64
+HALF = RANK // 2
 RHS = 8
 POINTS = 256
 CAPACITY = 16
@@ -57,8 +58,8 @@
     send_slot,
     far_target,
     out,
-    parent_raw,
-    leaf_raw,
+    raw,
+    turned,
     parent_w,
     leaf_w,
     near,
@@ -82,30 +83,36 @@
     me = lax.axis_index("clu")
     far_count = devices - NEAR
     group = far_count // GROUPS
-    load_rows = devices // LOADS
+    load_rows = HALF // LOADS
+    pair_count = 2 * devices
+
+    def wrap(index):
+        if devices & (devices - 1):
+            return lax.rem(index, devices)
+        return index & (devices - 1)
 
     def peer(j):
-        return lax.rem(me + (j - REACH + devices), devices)
+        return wrap(me + (j - REACH + devices))
 
     def tile_of(j):
         return 2 * j if j < NEAR else j + NEAR
 
-    parent_loads = [
-        pltpu.make_async_copy(
-            coupling.at[pl.ds(c * load_rows, load_rows), 1],
-            parent_raw.at[pl.ds(c * load_rows, load_rows)],
-            load_sem.at[c],
-        )
+    raw_loads = [
+        [
+            pltpu.make_async_copy(
+                coupling.at[pl.ds(first, load_rows)],
+                raw.at[pl.ds(first, load_rows)],
+                load_sem.at[c, h],
+            )
+            for h, first in enumerate((c * load_rows, HALF + c * load_rows))
+        ]
         for c in range(LOADS)
     ]
-    near_load = pltpu.make_async_copy(near_hbm, near, load_sem.at[LOADS + 1])
-    diag_load = pltpu.make_async_copy(diag_hbm, diag, load_sem.at[LOADS + 2])
-    for j in range(NEAR):
-        pltpu.make_async_copy(
-            coupling.at[peer(j), 0], leaf_raw.at[j], load_sem.at[LOADS]
-        ).start()
-    for load in parent_loads:
-        load.start()
+    near_load = pltpu.make_async_copy(near_hbm, near, load_sem.at[LOADS, 0])
+    diag_load = pltpu.make_async_copy(diag_hbm, diag, load_sem.at[LOADS, 1])
+    for loads in raw_loads:
+        for load in loads:
+            load.start()
     near_load.start()
     diag_load.start()
 
@@ -113,7 +120,7 @@
 
     def greet(step, carry):
         pl.semaphore_signal(
-            barrier, inc=1, device_id=(lax.rem(me + step, devices),), device_id_type=MESH
+            barrier, inc=1, device_id=(wrap(me + step),), device_id_type=MESH
         )
         return carry
 
@@ -140,45 +147,41 @@
             [own.astype(F32), nn(high, own) + nn(low, own)], axis=0
         ).astype(BF16)
 
+    def turn(k, carry):
+        both = jnp.concatenate([raw[k], raw[k + HALF]], axis=0)
+        turned[pl.ds(k, pair_count, stride=HALF), :] = both.T
+        return carry
+
+    for c in range(LOADS):
+        for load in raw_loads[c]:
+            load.wait()
+        lax.fori_loop(c * load_rows, (c + 1) * load_rows, turn, 0)
+
     lane = lax.broadcasted_iota(jnp.int32, (RANK, 2 * RANK), 1)
     row = lax.broadcasted_iota(jnp.int32, (RANK, 2 * RANK), 0)
     unit = jnp.where(lane == row + RANK, 1.0, 0.0)
     left = lane < RANK
 
-    def weights(raw, target, source, slots):
-        wide = jnp.where(left, jnp.concatenate([raw, raw], axis=1), unit)
-        slot = jnp.where(left, target, source)
+    def weights(column, slots):
+        low = turned[pl.ds(pl.multiple_of(column * HALF, HALF), HALF), :]
+        wide = jnp.where(left, jnp.concatenate([low, swap_halves(low)], axis=0), unit)
+        slot = jnp.where(left, far_target[0, column], send_slot[0, column])
         return [jnp.where(slot == s, wide, 0.0).astype(BF16) for s in slots]
 
-    pltpu.make_async_copy(leaf_raw, leaf_raw, load_sem.at[LOADS]).wait()
-
     def build_leaf(j, carry):
-        column = 2 * peer(j)
-        parts = weights(
-            leaf_raw[j], far_target[0, column], send_slot[0, column], range(LEAVES)
-        )
-        for s, part in enumerate(parts):
+        for s, part in enumerate(weights(2 * peer(j), range(LEAVES))):
             leaf_w[j, s * RANK : (s + 1) * RANK, :] = part
         return carry
 
     lax.fori_loop(0, NEAR, build_leaf, 0)
 
-    def build_parent(p, carry):
-        column = 2 * p + 1
-        parts = weights(
-            parent_raw[p],
-            far_target[0, column],
-            send_slot[0, column],
-            range(LEAVES, LEAVES + LEAVES // 2),
-        )
-        j = lax.rem(p - me + (REACH + devices), devices)
-        for s, part in enumerate(parts):
+    def build_parent(j, carry):
+        slots = range(LEAVES, LEAVES + LEAVES // 2)
+        for s, part in enumerate(weights(2 * peer(j) + 1, slots)):
             parent_w[j, s * RANK : (s + 1) * RANK, :] = part
         return carry
 
-    for c in range(LOADS):
-        parent_loads[c].wait()
-        lax.fori_loop(c * load_rows, (c + 1) * load_rows, build_parent, 0)
+    lax.fori_loop(0, devices, build_parent, 0, unroll=4)
 
     near_load.wait()
     diag_load.wait()
@@ -371,8 +374,8 @@
         ],
         out_specs=vmem,
         scratch_shapes=[
-            pltpu.VMEM((devices, RANK, RANK), F32),
-            pltpu.VMEM((NEAR, RANK, RANK), F32),
+            pltpu.VMEM((RANK, RANK, 2 * devices), F32),
+            pltpu.VMEM((2 * devices * HALF, 2 * RANK), F32),
             pltpu.VMEM((devices, 2 * RANK, 2 * RANK), BF16),
             pltpu.VMEM((NEAR, LEAVES * RANK, 2 * RANK), BF16),
             pltpu.VMEM((CAPACITY, POINTS, POINTS), BF16),
@@ -388,13 +391,13 @@
             pltpu.VMEM(sides, BF16),
             pltpu.VMEM(sides, BF16),
             pltpu.VMEM(sides, BF16),
-            pltpu.SemaphoreType.DMA((LOADS + 3,)),
+            pltpu.SemaphoreType.DMA((LOADS + 1, 2)),
             pltpu.SemaphoreType.DMA((PRODUCTS,)),
             pltpu.SemaphoreType.DMA((PRODUCTS, 1 + GROUPS)),
             pltpu.SemaphoreType.DMA((PRODUCTS, 4)),
         ],
         compiler_params=pltpu.CompilerParams(
-            collective_id=0, has_side_effects=True, vmem_limit_bytes=48 * 1024 * 1024
+            collective_id=0, has_side_effects=True, vmem_limit_bytes=61 * 1024 * 1024
         ),
         name="h2_products",
     )(
@@ -407,7 +410,7 @@
         near_second,
         leaf_basis,
         transfer,
-        coupling.reshape(devices, 2, RANK, RANK),
+        coupling.transpose(1, 2, 0),
         send_slot,
         far_target,
     )

time: 71.4 us -> 62.5 us (0.88)
  local copies, waits for them, and re-layouts: 10 us -> 1.57 us
    unnamed x22 -> x1, local copies, waits for them, and re-layouts: 10 us -> 1.57 us
where the time goes in v2:
time: 62.5 us; the launch traced here: 62.3 us
  Pallas kernels  60.1 us (96%)
  local copies, waits for them, and re-layouts  1.57 us (3%)
  between operations  0.66 us (1%)
    pallas_call x1, Pallas kernels, on_device(): pl.pallas_call(functools.partial(kernel, devices), out_shape=jax.ShapeDty...  60.1 us
    unnamed x1, local copies, waits for them, and re-layouts  1.57 us

profile of v2, /device:TPU:1, one launch (start us, length us, event | category | flops | bytes accessed | tf_op | source)
XLA Modules:
  0.0 62.3 jit_solution(1782198904961454370)
XLA Ops:
  0.7 60.1 %h2_products.1 = f32[4,4,8,256]{3,2,1,0:T(8,128)} custom-call(f32[4,8,256]{2,1,0:T(8,128)} %start.1, s32[4]{0:T(128)} %leaf_size.1, bf16[4,256,256]{2,1,0:T(8,128)(2,1)} %diag_hbm.1, bf16[16,256,256]{2,1,0:T(8,128)(2,1)} %near_hbm.1, s32[1]{0:T(128)S(6)} %copy.14.near_count, s32[16]{0:T(128)} %near_first.1, s32[16]{0:T(128)} %near_second.1, ...), custom_call_target="tpu_custom_call" | custom-call | tf_op jit(solution)/shard_map/h2_products/pallas_call | solution.py:358
  60.8 1.6 %copy.15 = f32[4,4,8,256]{3,2,1,0:T(8,128)} copy(f32[4,4,8,256]{3,2,1,0:T(8,128)} %h2_products.1) | data formatting | bytes 262144

commit v3 on v2

--- a/solution.py
+++ b/solution.py
@@ -18,6 +18,7 @@
 RHS = 8
 POINTS = 256
 CAPACITY = 16
+STRIDE = 4
 MESH = pl.DeviceIdType.MESH
 F32 = jnp.float32
 BF16 = jnp.bfloat16
@@ -35,8 +36,8 @@
     return pltpu.roll(a, RANK, 1)
 
 
-def pairs_of(first, last):
-    return [list(range(j, min(j + 2, last))) for j in range(first, last, 2)]
+def pairs_of(first, count):
+    return [[first + i for i in range(k, min(k + 2, count))] for k in range(0, count, 2)]
 
 
 def side_by_side(parts):
@@ -94,8 +95,14 @@
     def peer(j):
         return wrap(me + (j - REACH + devices))
 
-    def tile_of(j):
-        return 2 * j if j < NEAR else j + NEAR
+    def close_tile(j):
+        return 2 * j
+
+    def leaf_tile(j):
+        return 2 * j + 1
+
+    def far_tile(j):
+        return j + NEAR
 
     raw_loads = [
         [
@@ -155,7 +162,7 @@
     for c in range(LOADS):
         for load in raw_loads[c]:
             load.wait()
-        lax.fori_loop(c * load_rows, (c + 1) * load_rows, turn, 0)
+        lax.fori_loop(c * load_rows, (c + 1) * load_rows, turn, 0, unroll=4)
 
     lane = lax.broadcasted_iota(jnp.int32, (RANK, 2 * RANK), 1)
     row = lax.broadcasted_iota(jnp.int32, (RANK, 2 * RANK), 0)
@@ -181,7 +188,7 @@
             parent_w[j, s * RANK : (s + 1) * RANK, :] = part
         return carry
 
-    lax.fori_loop(0, devices, build_parent, 0, unroll=4)
+    lax.fori_loop(0, devices, build_parent, 0, unroll=8 if devices % 8 == 0 else 1)
 
     near_load.wait()
     diag_load.wait()
@@ -209,17 +216,21 @@
             near_out.at[n], near_in.at[n], side_sem.at[n, 2], side_sem.at[n, 3], peer(REACH + 1)
         )
 
-    def far_copy(n, j):
-        if j < NEAR:
-            src, dst, count, box = tile_of(j), tile_of(NEAR - 1 - j), 2, 0
-        else:
-            src, dst, count = tile_of(j), tile_of(devices + NEAR - 1 - j), 1
-            box = 1 + (j - NEAR) // group
+    def far_copy(n, j, g):
         return remote(
-            send.at[n, pl.ds(src, count)],
-            recv.at[n, pl.ds(dst, count)],
+            send.at[n, pl.ds(far_tile(j), 1)],
+            recv.at[n, pl.ds(far_tile(devices + NEAR - 1 - j), 1)],
             send_sem.at[n],
-            recv_sem.at[n, box],
+            recv_sem.at[n, 1 + g],
+            peer(j),
+        )
+
+    def close_copy(n, j):
+        return remote(
+            send.at[n, pl.ds(close_tile(j), 2)],
+            recv.at[n, pl.ds(close_tile(NEAR - 1 - j), 2)],
+            send_sem.at[n],
+            recv_sem.at[n, 0],
             peer(j),
         )
 
@@ -241,36 +252,50 @@
             half, swap_halves(coef[0] + coef[1]), coef[2] + coef[3]
         ).astype(BF16)
 
-        def fill(values, w, first, last, place):
-            for js in pairs_of(first, last):
+        def fill(values, w, first, count, place):
+            for js in pairs_of(first, count):
                 made = nn(values, side_by_side([w[j] for j in js]))
                 for i, j in enumerate(js):
                     tile = swap_halves(made[:, i * 2 * RANK : (i + 1) * 2 * RANK]).astype(BF16)
-                    if j == REACH:
+                    if isinstance(j, int) and j == REACH:
                         recv[n, place(j)] = tile
                     else:
                         send[n, place(j)] = tile
 
-        fill(leaf_coef, leaf_w, 0, NEAR, lambda j: tile_of(j) + 1)
-        fill(parent_coef, parent_w, 0, NEAR, tile_of)
+        fill(leaf_coef, leaf_w, 0, NEAR, leaf_tile)
+        fill(parent_coef, parent_w, 0, NEAR, close_tile)
         for j in range(NEAR):
             if j != REACH:
-                far_copy(n, j).start()
-        for g in range(GROUPS):
+                close_copy(n, j).start()
+
+        def send_group(g, carry):
             first = NEAR + g * group
-            fill(parent_coef, parent_w, first, first + group, tile_of)
-            for j in range(first, first + group):
-                far_copy(n, j).start()
+            fill(parent_coef, parent_w, first, group, far_tile)
+            for i in range(group):
+                far_copy(n, first + i, g).start()
+            return carry
+
+        lax.fori_loop(0, GROUPS, send_group, 0)
 
         for l in range(LEAVES):
             extended[l] = rounded[l].astype(F32)
-        backward = jnp.zeros((2 * LEAVES * RHS, POINTS), F32)
-        for e in range(CAPACITY):
-            own = extended[near_first[e]]
-            spread = jnp.concatenate(
-                [own * pick[e, LEAVES + s] for s in range(2 * LEAVES)], axis=0
-            ).astype(BF16)
-            backward = backward + nn(spread, near[e])
+
+        def add_backward(step, sofar):
+            for i in range(STRIDE):
+                e = step * STRIDE + i
+                own = extended[near_first[e]]
+                spread = jnp.concatenate(
+                    [own * pick[e, LEAVES + s] for s in range(2 * LEAVES)], axis=0
+                ).astype(BF16)
+                sofar = sofar + nn(spread, near[e])
+            return sofar
+
+        backward = lax.fori_loop(
+            0,
+            CAPACITY // STRIDE,
+            add_backward,
+            jnp.zeros((2 * LEAVES * RHS, POINTS), F32),
+        )
         near_out[n] = backward[LEAVES * RHS :].astype(BF16)
         near_copy(n).start()
         total = backward[: LEAVES * RHS] + jnp.concatenate(
@@ -281,15 +306,21 @@
         following = x_in[n].astype(F32)
         for l in range(LEAVES):
             extended[LEAVES + l] = following[l * RHS : (l + 1) * RHS]
-        for e in range(CAPACITY):
-            other = extended[near_second[e]]
-            spread = jnp.concatenate(
-                [other * pick[e, t] for t in range(LEAVES)], axis=0
-            ).astype(BF16)
-            total = total + nt(spread, near[e])
-
-        def take(w, first, last, place, sofar):
-            for js in pairs_of(first, last):
+
+        def add_forward(step, sofar):
+            for i in range(STRIDE):
+                e = step * STRIDE + i
+                other = extended[near_second[e]]
+                spread = jnp.concatenate(
+                    [other * pick[e, t] for t in range(LEAVES)], axis=0
+                ).astype(BF16)
+                sofar = sofar + nt(spread, near[e])
+            return sofar
+
+        total = lax.fori_loop(0, CAPACITY // STRIDE, add_forward, total)
+
+        def take(w, first, count, place, sofar):
+            for js in pairs_of(first, count):
                 got = side_by_side([recv[n, place(j)] for j in js])
                 sofar = sofar + nt(got, side_by_side([w[j] for j in js]))
             return sofar
@@ -300,13 +331,16 @@
 
         arrived(0, 2 * (NEAR - 1), 0)
         leaf_far = jnp.zeros((RHS, LEAVES * RANK), F32)
-        leaf_far = take(leaf_w, 0, NEAR, lambda j: tile_of(j) + 1, leaf_far)
+        leaf_far = take(leaf_w, 0, NEAR, leaf_tile, leaf_far)
         parent_far = jnp.zeros((RHS, 2 * RANK), F32)
-        parent_far = take(parent_w, 0, NEAR, tile_of, parent_far)
-        for g in range(GROUPS):
+        parent_far = take(parent_w, 0, NEAR, close_tile, parent_far)
+
+        def take_group(g, sofar):
             first = devices - (g + 1) * group
-            arrived(tile_of(first), group, 1 + g)
-            parent_far = take(parent_w, first, first + group, tile_of, parent_far)
+            arrived(far_tile(first), group, 1 + g)
+            return take(parent_w, first, group, far_tile, sofar)
+
+        parent_far = lax.fori_loop(0, GROUPS, take_group, parent_far)
 
         near_copy(n).wait_recv()
         total = total + near_in[n].astype(F32)
@@ -353,7 +387,7 @@
     tiles = devices + NEAR
     vmem = pl.BlockSpec(memory_space=pltpu.VMEM)
     smem = pl.BlockSpec(memory_space=pltpu.SMEM)
-    anywhere = pl.BlockSpec(memory_space=pl.ANY)
+    hbm = pl.BlockSpec(memory_space=pltpu.HBM)
     sides = (PRODUCTS, LEAVES * RHS, POINTS)
     return pl.pallas_call(
         functools.partial(kernel, devices),
@@ -361,14 +395,14 @@
         in_specs=[
             vmem,
             smem,
-            anywhere,
-            anywhere,
+            hbm,
+            hbm,
             smem,
             smem,
             smem,
             vmem,
             vmem,
-            anywhere,
+            hbm,
             smem,
             smem,
         ],
@@ -397,7 +431,7 @@
             pltpu.SemaphoreType.DMA((PRODUCTS, 4)),
         ],
         compiler_params=pltpu.CompilerParams(
-            collective_id=0, has_side_effects=True, vmem_limit_bytes=61 * 1024 * 1024
+            collective_id=0, has_side_effects=True, vmem_limit_bytes=56 * 1024 * 1024
         ),
         name="h2_products",
     )(

time: 62.5 us -> 57 us (0.912)
  Pallas kernels: 60.1 us -> 54.7 us
    pallas_call x1, Pallas kernels: 60.1 us -> 54.7 us  [on_device(): pl.pallas_call(functools.partial(kernel, devices), out_shape=jax.ShapeDty...]
where the time goes in v3:
time: 57 us; the launch traced here: 56.9 us
  Pallas kernels  54.7 us (96%)
  local copies, waits for them, and re-layouts  1.57 us (3%)
  between operations  0.66 us (1%)
    pallas_call x1, Pallas kernels, on_device(): pl.pallas_call(functools.partial(kernel, devices), out_shape=jax.ShapeDty...  54.7 us
    unnamed x1, local copies, waits for them, and re-layouts  1.57 us

profile of v3, /device:TPU:1, one launch (start us, length us, event | category | flops | bytes accessed | tf_op | source)
XLA Modules:
  0.0 56.9 jit_solution(12754710331784479157)
XLA Ops:
  0.7 54.7 %h2_products.1 = f32[4,4,8,256]{3,2,1,0:T(8,128)} custom-call(f32[4,8,256]{2,1,0:T(8,128)} %start.1, s32[4]{0:T(128)} %leaf_size.1, bf16[4,256,256]{2,1,0:T(8,128)(2,1)} %diag_hbm.1, bf16[16,256,256]{2,1,0:T(8,128)(2,1)} %near_hbm.1, s32[1]{0:T(128)S(6)} %copy.14.near_count, s32[16]{0:T(128)} %near_first.1, s32[16]{0:T(128)} %near_second.1, ...), custom_call_target="tpu_custom_call" | custom-call | tf_op jit(solution)/shard_map/h2_products/pallas_call | solution.py:392
  55.3 1.6 %copy.15 = f32[4,4,8,256]{3,2,1,0:T(8,128)} copy(f32[4,4,8,256]{3,2,1,0:T(8,128)} %h2_products.1) | data formatting | bytes 262144

commit v4 on v3

--- a/solution.py
+++ b/solution.py
@@ -9,8 +9,9 @@
 
 PRODUCTS = 4
 REACH = 8
-NEAR = 2 * REACH + 1
-GROUPS = 3
+CLOSE = REACH + 1
+NEAR = 2 * CLOSE
+GROUPS = 5
 LOADS = 4
 LEAVES = 4
 RANK = 64
@@ -34,10 +35,6 @@
 
 def swap_halves(a):
     return pltpu.roll(a, RANK, 1)
-
-
-def pairs_of(first, count):
-    return [[first + i for i in range(k, min(k + 2, count))] for k in range(0, count, 2)]
 
 
 def side_by_side(parts):
@@ -70,20 +67,28 @@
     point_mask,
     vector,
     extended,
-    send,
-    recv,
+    close_out,
+    far_out,
+    close_in,
+    far_in,
     x_out,
     x_in,
     near_out,
     near_in,
     load_sem,
+    hand_sem,
+    handed_sem,
     send_sem,
     recv_sem,
     side_sem,
 ):
     me = lax.axis_index("clu")
-    far_count = devices - NEAR
-    group = far_count // GROUPS
+    core = lax.rem(me, 2)
+    first_core = me - core
+    partner = first_core + 1 - core
+    chips = devices // 2
+    far_chips = chips - CLOSE
+    group = far_chips // GROUPS
     load_rows = HALF // LOADS
     pair_count = 2 * devices
 
@@ -92,17 +97,14 @@
             return lax.rem(index, devices)
         return index & (devices - 1)
 
-    def peer(j):
-        return wrap(me + (j - REACH + devices))
-
-    def close_tile(j):
-        return 2 * j
-
-    def leaf_tile(j):
-        return 2 * j + 1
-
-    def far_tile(j):
-        return j + NEAR
+    def at_position(j):
+        return wrap(first_core + (j - REACH + devices))
+
+    def peer(u):
+        return wrap(me + (2 * u - REACH + devices))
+
+    before = wrap(me + (devices - 1))
+    after = wrap(me + 1)
 
     raw_loads = [
         [
@@ -125,25 +127,22 @@
 
     barrier = pltpu.get_barrier_semaphore()
 
-    def greet(step, carry):
-        pl.semaphore_signal(
-            barrier, inc=1, device_id=(wrap(me + step),), device_id_type=MESH
-        )
+    def greet(target):
+        pl.semaphore_signal(barrier, inc=1, device_id=(target,), device_id_type=MESH)
+
+    def greet_chip(step, carry):
+        greet(wrap(me + 2 * step))
         return carry
 
-    lax.fori_loop(1, devices, greet, 0)
+    greet(before)
+    greet(after)
+    lax.fori_loop(1, chips, greet_chip, 0, unroll=9 if chips % 9 == 1 else 1)
 
     point_ids = lax.broadcasted_iota(jnp.int32, (RHS, POINTS), 1)
     for l in range(LEAVES):
         inside = jnp.where(point_ids < leaf_size[l], 1.0, 0.0)
         point_mask[l] = inside
         vector[l] = start[l] * inside
-    for e in range(CAPACITY):
-        live = e < near_count[0]
-        for t in range(LEAVES):
-            pick[e, t] = jnp.where(live & (near_first[e] == t), 1.0, 0.0)
-        for s in range(2 * LEAVES):
-            pick[e, LEAVES + s] = jnp.where(live & (near_second[e] == s), 1.0, 0.0)
 
     for l in range(LEAVES):
         moved = transfer[l].T
@@ -157,6 +156,12 @@
     def turn(k, carry):
         both = jnp.concatenate([raw[k], raw[k + HALF]], axis=0)
         turned[pl.ds(k, pair_count, stride=HALF), :] = both.T
+        e = k // 2
+        live = e < near_count[0]
+        for i in range(6):
+            column = 6 * (k % 2) + i
+            leaf = jnp.where(column < LEAVES, near_first[e], near_second[e] + LEAVES)
+            pick[e, column] = jnp.where(live & (leaf == column), 1.0, 0.0)
         return carry
 
     for c in range(LOADS):
@@ -176,15 +181,15 @@
         return [jnp.where(slot == s, wide, 0.0).astype(BF16) for s in slots]
 
     def build_leaf(j, carry):
-        for s, part in enumerate(weights(2 * peer(j), range(LEAVES))):
+        for s, part in enumerate(weights(2 * at_position(j), range(LEAVES))):
             leaf_w[j, s * RANK : (s + 1) * RANK, :] = part
         return carry
 
-    lax.fori_loop(0, NEAR, build_leaf, 0)
+    lax.fori_loop(0, NEAR, build_leaf, 0, unroll=2)
 
     def build_parent(j, carry):
         slots = range(LEAVES, LEAVES + LEAVES // 2)
-        for s, part in enumerate(weights(2 * peer(j) + 1, slots)):
+        for s, part in enumerate(weights(2 * at_position(j) + 1, slots)):
             parent_w[j, s * RANK : (s + 1) * RANK, :] = part
         return carry
 
@@ -192,7 +197,7 @@
 
     near_load.wait()
     diag_load.wait()
-    pl.semaphore_wait(barrier, devices - 1)
+    pl.semaphore_wait(barrier, chips + 1)
 
     half = lax.broadcasted_iota(jnp.int32, (RHS, 2 * RANK), 1) < RANK
 
@@ -208,31 +213,53 @@
 
     def x_copy(n):
         return remote(
-            x_out.at[n], x_in.at[n], side_sem.at[n, 0], side_sem.at[n, 1], peer(REACH - 1)
+            x_out.at[n], x_in.at[n], side_sem.at[n, 0], side_sem.at[n, 1], before
         )
 
     def near_copy(n):
         return remote(
-            near_out.at[n], near_in.at[n], side_sem.at[n, 2], side_sem.at[n, 3], peer(REACH + 1)
-        )
-
-    def far_copy(n, j, g):
+            near_out.at[n], near_in.at[n], side_sem.at[n, 2], side_sem.at[n, 3], after
+        )
+
+    def hand_close(n, level):
         return remote(
-            send.at[n, pl.ds(far_tile(j), 1)],
-            recv.at[n, pl.ds(far_tile(devices + NEAR - 1 - j), 1)],
-            send_sem.at[n],
+            close_out.at[n, :, 4 + level],
+            close_out.at[n, :, 2 * level + core],
+            hand_sem.at[n, 0],
+            handed_sem.at[n, 0],
+            partner,
+        )
+
+    def hand_far(n, g):
+        chips_of = pl.ds(g * group, group)
+        return remote(
+            far_out.at[n, chips_of, 2],
+            far_out.at[n, chips_of, core],
+            hand_sem.at[n, 1],
+            handed_sem.at[n, 1 + g],
+            partner,
+        )
+
+    def send_close(n, u):
+        return remote(
+            close_out.at[n, u, pl.ds(0, 4)],
+            close_in.at[n, CLOSE - 1 - u],
+            send_sem.at[n, 0],
+            recv_sem.at[n, 0],
+            peer(u),
+        )
+
+    def send_far(n, f, g):
+        return remote(
+            far_out.at[n, f, pl.ds(0, 2)],
+            far_in.at[n, far_chips - 1 - f],
+            send_sem.at[n, 1],
             recv_sem.at[n, 1 + g],
-            peer(j),
-        )
-
-    def close_copy(n, j):
-        return remote(
-            send.at[n, pl.ds(close_tile(j), 2)],
-            recv.at[n, pl.ds(close_tile(NEAR - 1 - j), 2)],
-            send_sem.at[n],
-            recv_sem.at[n, 0],
-            peer(j),
-        )
+            peer(f + CLOSE),
+        )
+
+    def wait_for(tiles, sem):
+        pltpu.make_async_copy(tiles, tiles, sem).wait()
 
     def product(n, carry):
         exact = [vector[l] for l in range(LEAVES)]
@@ -252,30 +279,45 @@
             half, swap_halves(coef[0] + coef[1]), coef[2] + coef[3]
         ).astype(BF16)
 
-        def fill(values, w, first, count, place):
-            for js in pairs_of(first, count):
-                made = nn(values, side_by_side([w[j] for j in js]))
-                for i, j in enumerate(js):
-                    tile = swap_halves(made[:, i * 2 * RANK : (i + 1) * 2 * RANK]).astype(BF16)
-                    if isinstance(j, int) and j == REACH:
-                        recv[n, place(j)] = tile
-                    else:
-                        send[n, place(j)] = tile
-
-        fill(leaf_coef, leaf_w, 0, NEAR, leaf_tile)
-        fill(parent_coef, parent_w, 0, NEAR, close_tile)
-        for j in range(NEAR):
-            if j != REACH:
-                close_copy(n, j).start()
-
-        def send_group(g, carry):
-            first = NEAR + g * group
-            fill(parent_coef, parent_w, first, group, far_tile)
+        def made(values, w, u):
+            both = nn(values, side_by_side([w[2 * u], w[2 * u + 1]]))
+            return [swap_halves(both[:, : 2 * RANK]), swap_halves(both[:, 2 * RANK :])]
+
+        for u in range(CLOSE):
+            for level, (values, w) in enumerate(
+                ((parent_coef, parent_w), (leaf_coef, leaf_w))
+            ):
+                first, second = made(values, w, u)
+                close_out[n, u, 2 * level + core * (4 - level)] = first.astype(BF16)
+                close_out[n, u, 4 + level - core * (3 - level)] = second.astype(BF16)
+        for level in range(2):
+            hand_close(n, level).start()
+
+        def fill_group(g):
             for i in range(group):
-                far_copy(n, first + i, g).start()
+                f = g * group + i
+                first, second = made(parent_coef, parent_w, f + CLOSE)
+                far_out[n, f, 2 * core] = first.astype(BF16)
+                far_out[n, f, 2 - core] = second.astype(BF16)
+            hand_far(n, g).start()
+
+        def send_group(g):
+            wait_for(far_out.at[n, pl.ds(g * group, group), 0], handed_sem.at[n, 1 + g])
+            for i in range(group):
+                send_far(n, g * group + i, g).start()
+
+        fill_group(0)
+        wait_for(close_out.at[n, :, pl.ds(0, 2)], handed_sem.at[n, 0])
+        for u in range(CLOSE):
+            if u != REACH // 2:
+                send_close(n, u).start()
+
+        def fill_and_send(g, carry):
+            fill_group(g)
+            send_group(g - 1)
             return carry
 
-        lax.fori_loop(0, GROUPS, send_group, 0)
+        lax.fori_loop(1, GROUPS, fill_and_send, 0)
 
         for l in range(LEAVES):
             extended[l] = rounded[l].astype(F32)
@@ -291,11 +333,10 @@
             return sofar
 
         backward = lax.fori_loop(
-            0,
-            CAPACITY // STRIDE,
-            add_backward,
-            jnp.zeros((2 * LEAVES * RHS, POINTS), F32),
-        )
+            0, 2, add_backward, jnp.zeros((2 * LEAVES * RHS, POINTS), F32)
+        )
+        send_group(GROUPS - 1)
+        backward = lax.fori_loop(2, CAPACITY // STRIDE, add_backward, backward)
         near_out[n] = backward[LEAVES * RHS :].astype(BF16)
         near_copy(n).start()
         total = backward[: LEAVES * RHS] + jnp.concatenate(
@@ -319,26 +360,28 @@
 
         total = lax.fori_loop(0, CAPACITY // STRIDE, add_forward, total)
 
-        def take(w, first, count, place, sofar):
-            for js in pairs_of(first, count):
-                got = side_by_side([recv[n, place(j)] for j in js])
-                sofar = sofar + nt(got, side_by_side([w[j] for j in js]))
+        def taken(tiles, w, u, sofar):
+            return sofar + nt(
+                side_by_side(tiles), side_by_side([w[2 * u], w[2 * u + 1]])
+            )
+
+        wait_for(close_in.at[n, pl.ds(0, CLOSE - 1)], recv_sem.at[n, 0])
+        leaf_far = jnp.zeros((RHS, LEAVES * RANK), F32)
+        parent_far = jnp.zeros((RHS, 2 * RANK), F32)
+        for u in range(CLOSE):
+            box = close_out if u == REACH // 2 else close_in
+            tiles = [box[n, u, s] for s in range(4)]
+            parent_far = taken(tiles[:2], parent_w, u, parent_far)
+            leaf_far = taken(tiles[2:], leaf_w, u, leaf_far)
+
+        def take_group(g, sofar):
+            first = far_chips - (g + 1) * group
+            wait_for(far_in.at[n, pl.ds(first, group)], recv_sem.at[n, 1 + g])
+            for i in range(group):
+                f = first + i
+                tiles = [far_in[n, f, s] for s in range(2)]
+                sofar = taken(tiles, parent_w, f + CLOSE, sofar)
             return sofar
-
-        def arrived(first, count, box):
-            tiles = recv.at[n, pl.ds(first, count)]
-            pltpu.make_async_copy(tiles, tiles, recv_sem.at[n, box]).wait()
-
-        arrived(0, 2 * (NEAR - 1), 0)
-        leaf_far = jnp.zeros((RHS, LEAVES * RANK), F32)
-        leaf_far = take(leaf_w, 0, NEAR, leaf_tile, leaf_far)
-        parent_far = jnp.zeros((RHS, 2 * RANK), F32)
-        parent_far = take(parent_w, 0, NEAR, close_tile, parent_far)
-
-        def take_group(g, sofar):
-            first = devices - (g + 1) * group
-            arrived(far_tile(first), group, 1 + g)
-            return take(parent_w, first, group, far_tile, sofar)
 
         parent_far = lax.fori_loop(0, GROUPS, take_group, parent_far)
 
@@ -360,8 +403,10 @@
     lax.fori_loop(0, PRODUCTS, product, 0)
 
     def finish(n, carry):
-        sent = send.at[n, pl.ds(0, 2 * (NEAR - 1) + far_count)]
-        pltpu.make_async_copy(sent, sent, send_sem.at[n]).wait()
+        wait_for(close_out.at[n, :, pl.ds(4, 2)], hand_sem.at[n, 0])
+        wait_for(far_out.at[n, :, 2], hand_sem.at[n, 1])
+        wait_for(close_out.at[n, pl.ds(0, CLOSE - 1), pl.ds(0, 4)], send_sem.at[n, 0])
+        wait_for(far_out.at[n, :, pl.ds(0, 2)], send_sem.at[n, 1])
         x_copy(n).wait_send()
         near_copy(n).wait_send()
         return carry
@@ -384,7 +429,8 @@
     far_target,
 ):
     devices = lax.axis_size("clu")
-    tiles = devices + NEAR
+    far_chips = devices // 2 - CLOSE
+    tile = (RHS, 2 * RANK)
     vmem = pl.BlockSpec(memory_space=pltpu.VMEM)
     smem = pl.BlockSpec(memory_space=pltpu.SMEM)
     hbm = pl.BlockSpec(memory_space=pltpu.HBM)
@@ -419,14 +465,18 @@
             pltpu.VMEM((LEAVES, RHS, POINTS), F32),
             pltpu.VMEM((LEAVES, RHS, POINTS), F32),
             pltpu.VMEM((2 * LEAVES, RHS, POINTS), F32),
-            pltpu.VMEM((PRODUCTS, tiles, RHS, 2 * RANK), BF16),
-            pltpu.VMEM((PRODUCTS, tiles, RHS, 2 * RANK), BF16),
+            pltpu.VMEM((PRODUCTS, CLOSE, 6, *tile), BF16),
+            pltpu.VMEM((PRODUCTS, far_chips, 3, *tile), BF16),
+            pltpu.VMEM((PRODUCTS, CLOSE, 4, *tile), BF16),
+            pltpu.VMEM((PRODUCTS, far_chips, 2, *tile), BF16),
             pltpu.VMEM(sides, BF16),
             pltpu.VMEM(sides, BF16),
             pltpu.VMEM(sides, BF16),
             pltpu.VMEM(sides, BF16),
             pltpu.SemaphoreType.DMA((LOADS + 1, 2)),
-            pltpu.SemaphoreType.DMA((PRODUCTS,)),
+            pltpu.SemaphoreType.DMA((PRODUCTS, 2)),
+            pltpu.SemaphoreType.DMA((PRODUCTS, 1 + GROUPS)),
+            pltpu.SemaphoreType.DMA((PRODUCTS, 2)),
             pltpu.SemaphoreType.DMA((PRODUCTS, 1 + GROUPS)),
             pltpu.SemaphoreType.DMA((PRODUCTS, 4)),
         ],

time: 57 us -> 61 us (1.070)
  Pallas kernels: 54.7 us -> 58.6 us
    pallas_call x1, Pallas kernels: 54.7 us -> 58.6 us  [on_device(): pl.pallas_call(functools.partial(kernel, devices), out_shape=jax.ShapeDty...]
where the time goes in v4:
time: 61 us; the launch traced here: 60.8 us
  Pallas kernels  58.6 us (96%)
  local copies, waits for them, and re-layouts  1.57 us (3%)
  between operations  0.66 us (1%)
    pallas_call x1, Pallas kernels, on_device(): pl.pallas_call(functools.partial(kernel, devices), out_shape=jax.ShapeDty...  58.6 us
    unnamed x1, local copies, waits for them, and re-layouts  1.57 us

profile of v4, /device:TPU:1, one launch (start us, length us, event | category | flops | bytes accessed | tf_op | source)
XLA Modules:
  0.0 60.8 jit_solution(12965391202859489654)
XLA Ops:
  0.7 58.6 %h2_products.1 = f32[4,4,8,256]{3,2,1,0:T(8,128)} custom-call(f32[4,8,256]{2,1,0:T(8,128)} %start.1, s32[4]{0:T(128)} %leaf_size.1, bf16[4,256,256]{2,1,0:T(8,128)(2,1)} %diag_hbm.1, bf16[16,256,256]{2,1,0:T(8,128)(2,1)} %near_hbm.1, s32[1]{0:T(128)S(6)} %copy.14.near_count, s32[16]{0:T(128)} %near_first.1, s32[16]{0:T(128)} %near_second.1, ...), custom_call_target="tpu_custom_call" | custom-call | tf_op jit(solution)/shard_map/h2_products/pallas_call | solution.py:438
  59.3 1.6 %copy.15 = f32[4,4,8,256]{3,2,1,0:T(8,128)} copy(f32[4,4,8,256]{3,2,1,0:T(8,128)} %h2_products.1) | data formatting | bytes 262144

commit v5 on v3

--- a/solution.py
+++ b/solution.py
@@ -1,4 +1,5 @@
 import functools
+import math
 
 import jax
 import jax.numpy as jnp
@@ -9,6 +10,7 @@
 
 PRODUCTS = 4
 REACH = 8
+CLOSE = REACH + 1
 NEAR = 2 * REACH + 1
 GROUPS = 3
 LOADS = 4
@@ -46,19 +48,22 @@
 
 def kernel(
     devices,
-    start,
+    start_hbm,
     leaf_size,
     diag_hbm,
     near_hbm,
     near_count,
     near_first,
     near_second,
-    basis,
-    transfer,
+    basis_hbm,
+    transfer_hbm,
     coupling,
     send_slot,
     far_target,
-    out,
+    out_hbm,
+    start,
+    basis,
+    transfer,
     raw,
     turned,
     parent_w,
@@ -69,6 +74,7 @@
     pick,
     point_mask,
     vector,
+    out,
     extended,
     send,
     recv,
@@ -77,6 +83,7 @@
     near_out,
     near_in,
     load_sem,
+    out_sem,
     send_sem,
     recv_sem,
     side_sem,
@@ -94,6 +101,9 @@
 
     def peer(j):
         return wrap(me + (j - REACH + devices))
+
+    def far_peer(g, i):
+        return wrap(me + (CLOSE + GROUPS * i) + g)
 
     def close_tile(j):
         return 2 * j
@@ -117,33 +127,39 @@
     ]
     near_load = pltpu.make_async_copy(near_hbm, near, load_sem.at[LOADS, 0])
     diag_load = pltpu.make_async_copy(diag_hbm, diag, load_sem.at[LOADS, 1])
+    small_loads = [
+        pltpu.make_async_copy(start_hbm, start, load_sem.at[LOADS + 1, 0]),
+        pltpu.make_async_copy(basis_hbm, basis, load_sem.at[LOADS + 1, 1]),
+        pltpu.make_async_copy(transfer_hbm, transfer, load_sem.at[LOADS + 2, 0]),
+    ]
     for loads in raw_loads:
         for load in loads:
             load.start()
+    for load in small_loads:
+        load.start()
     near_load.start()
     diag_load.start()
 
     barrier = pltpu.get_barrier_semaphore()
 
-    def greet(step, carry):
+    def greet(step):
         pl.semaphore_signal(
             barrier, inc=1, device_id=(wrap(me + step),), device_id_type=MESH
         )
-        return carry
-
-    lax.fori_loop(1, devices, greet, 0)
+
+    turns = HALF - load_rows
+    greetings = (devices - 1) // turns
+    for step in range(1 + turns * greetings, devices):
+        greet(step)
+
+    for load in small_loads:
+        load.wait()
 
     point_ids = lax.broadcasted_iota(jnp.int32, (RHS, POINTS), 1)
     for l in range(LEAVES):
         inside = jnp.where(point_ids < leaf_size[l], 1.0, 0.0)
         point_mask[l] = inside
         vector[l] = start[l] * inside
-    for e in range(CAPACITY):
-        live = e < near_count[0]
-        for t in range(LEAVES):
-            pick[e, t] = jnp.where(live & (near_first[e] == t), 1.0, 0.0)
-        for s in range(2 * LEAVES):
-            pick[e, LEAVES + s] = jnp.where(live & (near_second[e] == s), 1.0, 0.0)
 
     for l in range(LEAVES):
         moved = transfer[l].T
@@ -154,41 +170,65 @@
             [own.astype(F32), nn(high, own) + nn(low, own)], axis=0
         ).astype(BF16)
 
-    def turn(k, carry):
+    def turn(k, signals):
         both = jnp.concatenate([raw[k], raw[k + HALF]], axis=0)
         turned[pl.ds(k, pair_count, stride=HALF), :] = both.T
-        return carry
+        for i in range(signals):
+            greet(1 + signals * k + i)
+        e = k // 2
+        live = e < near_count[0]
+        for i in range(6):
+            column = 6 * (k % 2) + i
+            leaf = jnp.where(column < LEAVES, near_first[e], near_second[e] + LEAVES)
+            pick[e, column] = jnp.where(live & (leaf == column), 1.0, 0.0)
 
     for c in range(LOADS):
         for load in raw_loads[c]:
             load.wait()
-        lax.fori_loop(c * load_rows, (c + 1) * load_rows, turn, 0, unroll=4)
+        signals = greetings if c < LOADS - 1 else 0
+        lax.fori_loop(
+            c * load_rows,
+            (c + 1) * load_rows,
+            lambda k, carry: (turn(k, signals), carry)[1],
+            0,
+            unroll=4,
+        )
 
     lane = lax.broadcasted_iota(jnp.int32, (RANK, 2 * RANK), 1)
     row = lax.broadcasted_iota(jnp.int32, (RANK, 2 * RANK), 0)
-    unit = jnp.where(lane == row + RANK, 1.0, 0.0)
-    left = lane < RANK
-
-    def weights(column, slots):
+    unit = jnp.where(lane == row + RANK, 1.0, 0.0).astype(BF16)
+    left = lax.broadcasted_iota(jnp.int32, (2 * RHS, 2 * RANK), 1) < RANK
+
+    def repeated(mask):
+        return jnp.concatenate([mask.astype(BF16)] * (RANK // (2 * RHS)), axis=0)
+
+    def build(w, j, device, level, slots):
+        column = 2 * device + level
         low = turned[pl.ds(pl.multiple_of(column * HALF, HALF), HALF), :]
-        wide = jnp.where(left, jnp.concatenate([low, swap_halves(low)], axis=0), unit)
-        slot = jnp.where(left, far_target[0, column], send_slot[0, column])
-        return [jnp.where(slot == s, wide, 0.0).astype(BF16) for s in slots]
-
-    def build_leaf(j, carry):
-        for s, part in enumerate(weights(2 * peer(j), range(LEAVES))):
-            leaf_w[j, s * RANK : (s + 1) * RANK, :] = part
+        wide = jnp.concatenate([low, swap_halves(low)], axis=0).astype(BF16)
+        target, source = far_target[0, column], send_slot[0, column]
+        for i, s in enumerate(slots):
+            coupled = jnp.where(left, jnp.where(target == s, 1.0, 0.0), 0.0)
+            handed = jnp.where(left, 0.0, jnp.where(source == s, 1.0, 0.0))
+            w[j, i * RANK : (i + 1) * RANK, :] = wide * repeated(coupled) + unit * repeated(
+                handed
+            )
+
+    leaf_slots = range(LEAVES)
+    parent_slots = range(LEAVES, LEAVES + LEAVES // 2)
+
+    def build_near(j, carry):
+        build(leaf_w, j, peer(j), 0, leaf_slots)
+        build(parent_w, j, peer(j), 1, parent_slots)
         return carry
 
-    lax.fori_loop(0, NEAR, build_leaf, 0)
-
-    def build_parent(j, carry):
-        slots = range(LEAVES, LEAVES + LEAVES // 2)
-        for s, part in enumerate(weights(2 * peer(j) + 1, slots)):
-            parent_w[j, s * RANK : (s + 1) * RANK, :] = part
+    def build_far(i, carry):
+        for g in range(GROUPS):
+            build(parent_w, NEAR + g * group + i, far_peer(g, i), 1, parent_slots)
         return carry
 
-    lax.fori_loop(0, devices, build_parent, 0, unroll=8 if devices % 8 == 0 else 1)
+    lax.fori_loop(0, NEAR, build_near, 0)
+    lax.fori_loop(0, group, build_far, 0)
 
     near_load.wait()
     diag_load.wait()
@@ -216,13 +256,17 @@
             near_out.at[n], near_in.at[n], side_sem.at[n, 2], side_sem.at[n, 3], peer(REACH + 1)
         )
 
-    def far_copy(n, j, g):
+    def out_copy(n):
+        return pltpu.make_async_copy(out.at[n], out_hbm.at[n], out_sem.at[n])
+
+    def far_copy(n, g, i):
+        w = g * group + i
         return remote(
-            send.at[n, pl.ds(far_tile(j), 1)],
-            recv.at[n, pl.ds(far_tile(devices + NEAR - 1 - j), 1)],
+            send.at[n, pl.ds(2 * NEAR + w, 1)],
+            recv.at[n, pl.ds(2 * NEAR + far_count - 1 - w, 1)],
             send_sem.at[n],
             recv_sem.at[n, 1 + g],
-            peer(j),
+            far_peer(g, i),
         )
 
     def close_copy(n, j):
@@ -233,6 +277,9 @@
             recv_sem.at[n, 0],
             peer(j),
         )
+
+    spread_by = next(k for k in range(3 * group // 8, group + 2) if k and math.gcd(k, group) == 1)
+    order = [i * spread_by % group for i in range(group)]
 
     def product(n, carry):
         exact = [vector[l] for l in range(LEAVES)]
@@ -252,30 +299,52 @@
             half, swap_halves(coef[0] + coef[1]), coef[2] + coef[3]
         ).astype(BF16)
 
-        def fill(values, w, first, count, place):
-            for js in pairs_of(first, count):
-                made = nn(values, side_by_side([w[j] for j in js]))
-                for i, j in enumerate(js):
-                    tile = swap_halves(made[:, i * 2 * RANK : (i + 1) * 2 * RANK]).astype(BF16)
-                    if isinstance(j, int) and j == REACH:
-                        recv[n, place(j)] = tile
-                    else:
-                        send[n, place(j)] = tile
-
-        fill(leaf_coef, leaf_w, 0, NEAR, leaf_tile)
-        fill(parent_coef, parent_w, 0, NEAR, close_tile)
+        def fill(values, w, js, place):
+            made = nn(values, side_by_side([w[j] for j in js]))
+            for i, j in enumerate(js):
+                tile = swap_halves(made[:, i * 2 * RANK : (i + 1) * 2 * RANK]).astype(BF16)
+                if isinstance(j, int) and j == REACH:
+                    recv[n, place(j)] = tile
+                else:
+                    send[n, place(j)] = tile
+
+        def far_fills(g):
+            return [
+                functools.partial(fill, parent_coef, parent_w, js, far_tile)
+                for js in pairs_of(NEAR + g * group, group)
+            ]
+
+        def interleave(fills, g):
+            done = 0
+            for k, step in enumerate(fills):
+                step()
+                upto = (k + 1) * group // len(fills)
+                for i in order[done:upto]:
+                    far_copy(n, g, i).start()
+                done = upto
+
+        for step in far_fills(0):
+            step()
+
+        def fill_next(g, carry):
+            interleave(far_fills(g), g - 1)
+            return carry
+
+        lax.fori_loop(1, GROUPS, fill_next, 0)
+        interleave(
+            [
+                functools.partial(fill, values, w, js, place)
+                for js in pairs_of(0, NEAR)
+                for values, w, place in (
+                    (parent_coef, parent_w, close_tile),
+                    (leaf_coef, leaf_w, leaf_tile),
+                )
+            ],
+            GROUPS - 1,
+        )
         for j in range(NEAR):
             if j != REACH:
                 close_copy(n, j).start()
-
-        def send_group(g, carry):
-            first = NEAR + g * group
-            fill(parent_coef, parent_w, first, group, far_tile)
-            for i in range(group):
-                far_copy(n, first + i, g).start()
-            return carry
-
-        lax.fori_loop(0, GROUPS, send_group, 0)
 
         for l in range(LEAVES):
             extended[l] = rounded[l].astype(F32)
@@ -355,6 +424,7 @@
             value = value * point_mask[l]
             vector[l] = value
             out[n, l] = value
+        out_copy(n).start()
         return carry
 
     lax.fori_loop(0, PRODUCTS, product, 0)
@@ -364,6 +434,7 @@
         pltpu.make_async_copy(sent, sent, send_sem.at[n]).wait()
         x_copy(n).wait_send()
         near_copy(n).wait_send()
+        out_copy(n).wait()
         return carry
 
     lax.fori_loop(0, PRODUCTS, finish, 0)
@@ -385,7 +456,6 @@
 ):
     devices = lax.axis_size("clu")
     tiles = devices + NEAR
-    vmem = pl.BlockSpec(memory_space=pltpu.VMEM)
     smem = pl.BlockSpec(memory_space=pltpu.SMEM)
     hbm = pl.BlockSpec(memory_space=pltpu.HBM)
     sides = (PRODUCTS, LEAVES * RHS, POINTS)
@@ -393,21 +463,24 @@
         functools.partial(kernel, devices),
         out_shape=jax.ShapeDtypeStruct((PRODUCTS, LEAVES, RHS, POINTS), F32),
         in_specs=[
-            vmem,
+            hbm,
             smem,
             hbm,
             hbm,
             smem,
             smem,
             smem,
-            vmem,
-            vmem,
+            hbm,
+            hbm,
             hbm,
             smem,
             smem,
         ],
-        out_specs=vmem,
+        out_specs=hbm,
         scratch_shapes=[
+            pltpu.VMEM((LEAVES, RHS, POINTS), F32),
+            pltpu.VMEM((LEAVES, RANK, POINTS), BF16),
+            pltpu.VMEM((LEAVES, RANK, RANK), F32),
             pltpu.VMEM((RANK, RANK, 2 * devices), F32),
             pltpu.VMEM((2 * devices * HALF, 2 * RANK), F32),
             pltpu.VMEM((devices, 2 * RANK, 2 * RANK), BF16),
@@ -418,6 +491,7 @@
             pltpu.SMEM((CAPACITY, 3 * LEAVES), F32),
             pltpu.VMEM((LEAVES, RHS, POINTS), F32),
             pltpu.VMEM((LEAVES, RHS, POINTS), F32),
+            pltpu.VMEM((PRODUCTS, LEAVES, RHS, POINTS), F32),
             pltpu.VMEM((2 * LEAVES, RHS, POINTS), F32),
             pltpu.VMEM((PRODUCTS, tiles, RHS, 2 * RANK), BF16),
             pltpu.VMEM((PRODUCTS, tiles, RHS, 2 * RANK), BF16),
@@ -425,7 +499,8 @@
             pltpu.VMEM(sides, BF16),
             pltpu.VMEM(sides, BF16),
             pltpu.VMEM(sides, BF16),
-            pltpu.SemaphoreType.DMA((LOADS + 1, 2)),
+            pltpu.SemaphoreType.DMA((LOADS + 3, 2)),
+            pltpu.SemaphoreType.DMA((PRODUCTS,)),
             pltpu.SemaphoreType.DMA((PRODUCTS,)),
             pltpu.SemaphoreType.DMA((PRODUCTS, 1 + GROUPS)),
             pltpu.SemaphoreType.DMA((PRODUCTS, 4)),

time: 57 us -> 101 us (1.77)
  Pallas kernels: 54.7 us -> 98.8 us
    pallas_call x1, Pallas kernels: 54.7 us -> 98.8 us  [on_device(): pl.pallas_call(functools.partial(kernel, devices), out_shape=jax.ShapeDty...]
where the time goes in v5:
time: 101 us
  Pallas kernels  98.8 us (98%)
  local copies, waits for them, and re-layouts  1.57 us (2%)
    pallas_call x1, Pallas kernels, on_device(): pl.pallas_call(functools.partial(kernel, devices), out_shape=jax.ShapeDty...  98.8 us

profile of v5, /device:TPU:1, one launch (start us, length us, event | category | flops | bytes accessed | tf_op | source)
XLA Modules:
  0.0 101.0 jit_solution(16114217048477757710)
XLA Ops:
  0.7 98.8 %h2_products.1 = f32[4,4,8,256]{3,2,1,0:T(8,128)} custom-call(f32[4,8,256]{2,1,0:T(8,128)} %start_hbm.1, s32[4]{0:T(128)} %leaf_size.1, bf16[4,256,256]{2,1,0:T(8,128)(2,1)} %diag_hbm.1, bf16[16,256,256]{2,1,0:T(8,128)(2,1)} %near_hbm.1, s32[1]{0:T(128)S(6)} %copy.14.near_count, s32[16]{0:T(128)} %near_first.1, s32[16]{0:T(128)} %near_second.1, ...), custom_call_target="tpu_custom_call" | custom-call | tf_op jit(solution)/shard_map/h2_products/pallas_call | solution.py:462
  99.4 1.6 %copy.15 = f32[4,4,8,256]{3,2,1,0:T(8,128)} copy(f32[4,4,8,256]{3,2,1,0:T(8,128)} %h2_products.1) | data formatting | bytes 262144

commit v6 on v5

--- a/solution.py
+++ b/solution.py
@@ -142,15 +142,13 @@
 
     barrier = pltpu.get_barrier_semaphore()
 
-    def greet(step):
+    def greet(step, carry):
         pl.semaphore_signal(
             barrier, inc=1, device_id=(wrap(me + step),), device_id_type=MESH
         )
-
-    turns = HALF - load_rows
-    greetings = (devices - 1) // turns
-    for step in range(1 + turns * greetings, devices):
-        greet(step)
+        return carry
+
+    lax.fori_loop(1, devices, greet, 0)
 
     for load in small_loads:
         load.wait()
@@ -170,29 +168,21 @@
             [own.astype(F32), nn(high, own) + nn(low, own)], axis=0
         ).astype(BF16)
 
-    def turn(k, signals):
+    def turn(k, carry):
         both = jnp.concatenate([raw[k], raw[k + HALF]], axis=0)
         turned[pl.ds(k, pair_count, stride=HALF), :] = both.T
-        for i in range(signals):
-            greet(1 + signals * k + i)
         e = k // 2
         live = e < near_count[0]
         for i in range(6):
             column = 6 * (k % 2) + i
             leaf = jnp.where(column < LEAVES, near_first[e], near_second[e] + LEAVES)
             pick[e, column] = jnp.where(live & (leaf == column), 1.0, 0.0)
+        return carry
 
     for c in range(LOADS):
         for load in raw_loads[c]:
             load.wait()
-        signals = greetings if c < LOADS - 1 else 0
-        lax.fori_loop(
-            c * load_rows,
-            (c + 1) * load_rows,
-            lambda k, carry: (turn(k, signals), carry)[1],
-            0,
-            unroll=4,
-        )
+        lax.fori_loop(c * load_rows, (c + 1) * load_rows, turn, 0, unroll=4)
 
     lane = lax.broadcasted_iota(jnp.int32, (RANK, 2 * RANK), 1)
     row = lax.broadcasted_iota(jnp.int32, (RANK, 2 * RANK), 0)
@@ -299,49 +289,25 @@
             half, swap_halves(coef[0] + coef[1]), coef[2] + coef[3]
         ).astype(BF16)
 
-        def fill(values, w, js, place):
-            made = nn(values, side_by_side([w[j] for j in js]))
-            for i, j in enumerate(js):
-                tile = swap_halves(made[:, i * 2 * RANK : (i + 1) * 2 * RANK]).astype(BF16)
-                if isinstance(j, int) and j == REACH:
-                    recv[n, place(j)] = tile
-                else:
-                    send[n, place(j)] = tile
-
-        def far_fills(g):
-            return [
-                functools.partial(fill, parent_coef, parent_w, js, far_tile)
-                for js in pairs_of(NEAR + g * group, group)
-            ]
-
-        def interleave(fills, g):
-            done = 0
-            for k, step in enumerate(fills):
-                step()
-                upto = (k + 1) * group // len(fills)
-                for i in order[done:upto]:
-                    far_copy(n, g, i).start()
-                done = upto
-
-        for step in far_fills(0):
-            step()
-
-        def fill_next(g, carry):
-            interleave(far_fills(g), g - 1)
+        def fill(values, w, first, count, place):
+            for js in pairs_of(first, count):
+                made = nn(values, side_by_side([w[j] for j in js]))
+                for i, j in enumerate(js):
+                    tile = swap_halves(made[:, i * 2 * RANK : (i + 1) * 2 * RANK]).astype(BF16)
+                    if isinstance(j, int) and j == REACH:
+                        recv[n, place(j)] = tile
+                    else:
+                        send[n, place(j)] = tile
+
+        def send_group(g, carry):
+            fill(parent_coef, parent_w, NEAR + g * group, group, far_tile)
+            for i in order:
+                far_copy(n, g, i).start()
             return carry
 
-        lax.fori_loop(1, GROUPS, fill_next, 0)
-        interleave(
-            [
-                functools.partial(fill, values, w, js, place)
-                for js in pairs_of(0, NEAR)
-                for values, w, place in (
-                    (parent_coef, parent_w, close_tile),
-                    (leaf_coef, leaf_w, leaf_tile),
-                )
-            ],
-            GROUPS - 1,
-        )
+        lax.fori_loop(0, GROUPS, send_group, 0)
+        fill(parent_coef, parent_w, 0, NEAR, close_tile)
+        fill(leaf_coef, leaf_w, 0, NEAR, leaf_tile)
         for j in range(NEAR):
             if j != REACH:
                 close_copy(n, j).start()

time: 101 us -> 62.1 us (0.61)
  Pallas kernels: 98.8 us -> 59.7 us
    pallas_call x1, Pallas kernels: 98.8 us -> 59.7 us  [on_device(): pl.pallas_call(functools.partial(kernel, devices), out_shape=jax.ShapeDty...]
where the time goes in v6:
time: 62.1 us; the launch traced here: 61.9 us
  Pallas kernels  59.7 us (96%)
  local copies, waits for them, and re-layouts  1.57 us (3%)
  between operations  0.66 us (1%)
    pallas_call x1, Pallas kernels, on_device(): pl.pallas_call(functools.partial(kernel, devices), out_shape=jax.ShapeDty...  59.7 us
    unnamed x1, local copies, waits for them, and re-layouts  1.57 us

profile of v6, /device:TPU:1, one launch (start us, length us, event | category | flops | bytes accessed | tf_op | source)
XLA Modules:
  0.0 61.9 jit_solution(3939413298460936947)
XLA Ops:
  0.7 59.7 %h2_products.1 = f32[4,4,8,256]{3,2,1,0:T(8,128)} custom-call(f32[4,8,256]{2,1,0:T(8,128)} %start_hbm.1, s32[4]{0:T(128)} %leaf_size.1, bf16[4,256,256]{2,1,0:T(8,128)(2,1)} %diag_hbm.1, bf16[16,256,256]{2,1,0:T(8,128)(2,1)} %near_hbm.1, s32[1]{0:T(128)S(6)} %copy.14.near_count, s32[16]{0:T(128)} %near_first.1, s32[16]{0:T(128)} %near_second.1, ...), custom_call_target="tpu_custom_call" | custom-call | tf_op jit(solution)/shard_map/h2_products/pallas_call | solution.py:428
  60.4 1.6 %copy.15 = f32[4,4,8,256]{3,2,1,0:T(8,128)} copy(f32[4,4,8,256]{3,2,1,0:T(8,128)} %h2_products.1) | data formatting | bytes 262144

commit v7 on v6

v7 whole, which is shorter than its diff:
```python
import functools

import jax
import jax.numpy as jnp
from jax import lax
from jax.experimental import pallas as pl
from jax.experimental.pallas import tpu as pltpu
from jax.sharding import PartitionSpec as P

PRODUCTS = 4
REACH = 8
CLOSE = 2 * REACH + 1
GROUPS = 4
STEP = 37
LOADS = 4
LEAVES = 4
PARENTS = LEAVES // 2
RANK = 64
HALF = RANK // 2
RHS = 8
POINTS = 256
CAPACITY = 16
STRIDE = 4
MESH = pl.DeviceIdType.MESH
F32 = jnp.float32
BF16 = jnp.bfloat16


def nn(a, b):
    return jnp.dot(a, b, preferred_element_type=F32)


def nt(a, b):
    return lax.dot_general(a, b, (((1,), (1,)), ((), ())), preferred_element_type=F32)


def swap_halves(a):
    return pltpu.roll(a, RANK, 1)


def side_by_side(parts):
    return parts[0] if len(parts) == 1 else jnp.concatenate(parts, axis=1)


def kernel(
    devices,
    start_hbm,
    leaf_size,
    diag_hbm,
    near_hbm,
    near_count,
    near_first,
    near_second,
    basis_hbm,
    transfer_hbm,
    coupling,
    send_slot,
    far_target,
    out_hbm,
    start,
    basis,
    transfer,
    raw,
    turned,
    parent_w,
    leaf_w,
    parent_slots,
    leaf_slots,
    near,
    diag,
    both_basis,
    pick,
    point_mask,
    vector,
    out,
    extended,
    send,
    recv,
    leaf_send,
    leaf_recv,
    x_out,
    x_in,
    near_out,
    near_in,
    load_sem,
    out_sem,
    send_sem,
    recv_sem,
    side_sem,
):
    me = lax.axis_index("clu")
    group = devices // GROUPS
    load_rows = HALF // LOADS
    pair_count = 2 * devices

    def wrap(index):
        if devices & (devices - 1):
            return lax.rem(index, devices)
        return index & (devices - 1)

    def partner(w):
        return wrap(me + STEP * (w + 1))

    def leaf_partner(v):
        return wrap(me + (v - REACH + devices))

    raw_loads = [
        [
            pltpu.make_async_copy(
                coupling.at[pl.ds(first, load_rows)],
                raw.at[pl.ds(first, load_rows)],
                load_sem.at[c, h],
            )
            for h, first in enumerate((c * load_rows, HALF + c * load_rows))
        ]
        for c in range(LOADS)
    ]
    near_load = pltpu.make_async_copy(near_hbm, near, load_sem.at[LOADS, 0])
    diag_load = pltpu.make_async_copy(diag_hbm, diag, load_sem.at[LOADS, 1])
    small_loads = [
        pltpu.make_async_copy(start_hbm, start, load_sem.at[LOADS + 1, 0]),
        pltpu.make_async_copy(basis_hbm, basis, load_sem.at[LOADS + 1, 1]),
        pltpu.make_async_copy(transfer_hbm, transfer, load_sem.at[LOADS + 2, 0]),
    ]
    for loads in raw_loads:
        for load in loads:
            load.start()
    for load in small_loads:
        load.start()
    near_load.start()
    diag_load.start()

    barrier = pltpu.get_barrier_semaphore()

    def greet(step, carry):
        pl.semaphore_signal(
            barrier, inc=1, device_id=(wrap(me + step),), device_id_type=MESH
        )
        return carry

    lax.fori_loop(1, devices, greet, 0)

    for load in small_loads:
        load.wait()

    point_ids = lax.broadcasted_iota(jnp.int32, (RHS, POINTS), 1)
    for l in range(LEAVES):
        inside = jnp.where(point_ids < leaf_size[l], 1.0, 0.0)
        point_mask[l] = inside
        vector[l] = start[l] * inside

    for l in range(LEAVES):
        moved = transfer[l].T
        high = moved.astype(BF16)
        low = (moved - high.astype(F32)).astype(BF16)
        own = basis[l]
        both_basis[l] = jnp.concatenate(
            [nn(high, own) + nn(low, own), own.astype(F32)], axis=0
        ).astype(BF16)

    def turn(k, carry):
        both = jnp.concatenate([raw[k], raw[k + HALF]], axis=0)
        turned[pl.ds(k, pair_count, stride=HALF), :] = both.T
        e = k // 2
        live = e < near_count[0]
        for i in range(6):
            column = 6 * (k % 2) + i
            leaf = jnp.where(column < LEAVES, near_first[e], near_second[e] + LEAVES)
            pick[e, column] = jnp.where(live & (leaf == column), 1.0, 0.0)
        return carry

    for c in range(LOADS):
        for load in raw_loads[c]:
            load.wait()
        lax.fori_loop(c * load_rows, (c + 1) * load_rows, turn, 0, unroll=4)

    left = lax.broadcasted_iota(jnp.int32, (RHS, 2 * RANK), 1) < RANK

    def on_left(rows):
        return jnp.concatenate([left] * (rows // RHS), axis=0)

    def build(w, slots, u, first, second):
        tiles = [
            turned[pl.ds(pl.multiple_of(column * HALF, HALF), HALF), :]
            for column in (first, second)
        ]
        swapped = [swap_halves(tile) for tile in tiles]
        w[u] = jnp.concatenate(
            [
                jnp.where(on_left(HALF), tiles[0], swapped[1]),
                jnp.where(on_left(HALF), swapped[0], tiles[1]),
            ],
            axis=0,
        ).astype(BF16)
        slots[u, 0] = jnp.where(left, far_target[0, first], far_target[0, second])
        slots[u, 1] = jnp.where(left, send_slot[0, first], send_slot[0, second])
        slots[u, 2] = jnp.where(left, send_slot[0, second], send_slot[0, first])

    def build_parent(u, carry):
        build(
            parent_w, parent_slots, u, 2 * partner(2 * u) + 1, 2 * partner(2 * u + 1) + 1
        )
        return carry

    def build_leaf(u, carry):
        build(leaf_w, leaf_slots, u, 2 * leaf_partner(2 * u), 2 * leaf_partner(2 * u + 1))
        return carry

    lax.fori_loop(0, devices // 2, build_parent, 0, unroll=8)
    lax.fori_loop(0, (CLOSE + 1) // 2, build_leaf, 0, unroll=3)
    for n in range(PRODUCTS):
        leaf_recv[n, CLOSE] = jnp.zeros((RHS, 2 * RANK), BF16)

    near_load.wait()
    diag_load.wait()
    pl.semaphore_wait(barrier, devices - 1)

    def remote(src, dst, out_sem, in_sem, target):
        return pltpu.make_async_remote_copy(
            src_ref=src,
            dst_ref=dst,
            send_sem=out_sem,
            recv_sem=in_sem,
            device_id=(target,),
            device_id_type=MESH,
        )

    def x_copy(n):
        return remote(
            x_out.at[n], x_in.at[n], side_sem.at[n, 0], side_sem.at[n, 1], leaf_partner(REACH - 1)
        )

    def near_copy(n):
        return remote(
            near_out.at[n], near_in.at[n], side_sem.at[n, 2], side_sem.at[n, 3], leaf_partner(REACH + 1)
        )

    def out_copy(n):
        return pltpu.make_async_copy(out.at[n], out_hbm.at[n], out_sem.at[n])

    def parent_copy(n, g, i):
        w = g * group + i
        return remote(
            send.at[n, pl.ds(w, 1)],
            recv.at[n, pl.ds(devices - 2 - w, 1)],
            send_sem.at[n, 0],
            recv_sem.at[n, g],
            partner(w),
        )

    def leaf_copy(n, v):
        return remote(
            leaf_send.at[n, pl.ds(v, 1)],
            leaf_recv.at[n, pl.ds(2 * REACH - v, 1)],
            send_sem.at[n, 1],
            recv_sem.at[n, GROUPS],
            leaf_partner(v),
        )

    def wait_for(tiles, sem):
        pltpu.make_async_copy(tiles, tiles, sem).wait()

    def chosen(slot, rows, first):
        count = rows.shape[0] // RHS
        result = rows[(count - 1) * RHS :]
        for t in reversed(range(count - 1)):
            result = jnp.where(slot == first + t, rows[t * RHS : (t + 1) * RHS], result)
        return result

    def kept(slot, value, first, count):
        return jnp.concatenate(
            [jnp.where(slot == first + t, value, 0.0) for t in range(count)], axis=0
        )

    def twos(first, count):
        return [[first + i for i in range(k, min(k + 2, count))] for k in range(0, count, 2)]

    def product(n, carry):
        exact = [vector[l] for l in range(LEAVES)]
        rounded = [value.astype(BF16) for value in exact]
        x_out[n] = jnp.concatenate(exact, axis=0).astype(BF16)
        x_copy(n).start()

        coef = [nt(rounded[l], both_basis[l]) for l in range(LEAVES)]
        parent = jnp.concatenate(
            [coef[2 * q] + coef[2 * q + 1] for q in range(PARENTS)], axis=0
        )
        leaf = jnp.concatenate(coef, axis=0)
        leaf_turned = swap_halves(leaf)
        parent_twice = jnp.where(on_left(PARENTS * RHS), parent, swap_halves(parent))
        leaf_twice = jnp.where(on_left(LEAVES * RHS), leaf_turned, leaf)
        parent_rows = parent[:, :RANK].astype(BF16)
        leaf_rows = leaf_turned[:, :RANK].astype(BF16)

        def fill(rows, twice, w, slots, first_slot, first, count, store):
            for us in twos(first, count):
                made = nn(rows, side_by_side([w[u] for u in us]))
                for i, u in enumerate(us):
                    block = made[:, i * 2 * RANK : (i + 1) * 2 * RANK]
                    outward = swap_halves(chosen(slots[u, 0], block, first_slot))
                    own = chosen(slots[u, 1], twice, first_slot)
                    store(2 * u, jnp.where(left, own, outward).astype(BF16))
                    store(2 * u + 1, jnp.where(left, outward, own).astype(BF16))

        def store_parent(w, tile):
            if isinstance(w, int) and w == devices - 1:
                recv[n, w] = tile
            else:
                send[n, w] = tile

        def store_leaf(v, tile):
            if v == REACH:
                leaf_recv[n, v] = tile
            elif v < CLOSE:
                leaf_send[n, v] = tile

        def send_group(g, count):
            fill(
                parent_rows,
                parent_twice,
                parent_w,
                parent_slots,
                LEAVES,
                g * (group // 2),
                group // 2,
                store_parent,
            )
            for i in range(count):
                parent_copy(n, g, i).start()

        def send_whole_group(g, carry):
            send_group(g, group)
            return carry

        lax.fori_loop(0, GROUPS - 1, send_whole_group, 0)
        send_group(GROUPS - 1, group - 1)
        fill(
            leaf_rows, leaf_twice, leaf_w, leaf_slots, 0, 0, (CLOSE + 1) // 2, store_leaf
        )
        for v in range(CLOSE):
            if v != REACH:
                leaf_copy(n, v).start()

        for l in range(LEAVES):
            extended[l] = rounded[l].astype(F32)

        def add_backward(step, sofar):
            for i in range(STRIDE):
                e = step * STRIDE + i
                own = extended[near_first[e]]
                spread = jnp.concatenate(
                    [own * pick[e, LEAVES + s] for s in range(2 * LEAVES)], axis=0
                ).astype(BF16)
                sofar = sofar + nn(spread, near[e])
            return sofar

        backward = lax.fori_loop(
            0,
            CAPACITY // STRIDE,
            add_backward,
            jnp.zeros((2 * LEAVES * RHS, POINTS), F32),
        )
        near_out[n] = backward[LEAVES * RHS :].astype(BF16)
        near_copy(n).start()
        total = backward[: LEAVES * RHS] + jnp.concatenate(
            [nn(rounded[l], diag[l]) for l in range(LEAVES)], axis=0
        )

        x_copy(n).wait_recv()
        following = x_in[n].astype(F32)
        for l in range(LEAVES):
            extended[LEAVES + l] = following[l * RHS : (l + 1) * RHS]

        def add_forward(step, sofar):
            for i in range(STRIDE):
                e = step * STRIDE + i
                other = extended[near_second[e]]
                spread = jnp.concatenate(
                    [other * pick[e, t] for t in range(LEAVES)], axis=0
                ).astype(BF16)
                sofar = sofar + nt(spread, near[e])
            return sofar

        total = lax.fori_loop(0, CAPACITY // STRIDE, add_forward, total)

        def take(box, w, slots, first_slot, slot_count, first, count, sofar):
            through, handed = sofar
            for us in twos(first, count):
                rows = []
                for u in us:
                    even, odd = box[n, 2 * u].astype(F32), box[n, 2 * u + 1].astype(F32)
                    incoming = jnp.where(left, even, odd)
                    outcome = jnp.where(left, odd, even)
                    rows.append(kept(slots[u, 0], incoming, first_slot, slot_count))
                    handed = handed + kept(slots[u, 2], outcome, first_slot, slot_count)
                through = through + nt(
                    side_by_side(rows).astype(BF16), side_by_side([w[u] for u in us])
                )
            return through, handed

        def nothing(count):
            return (
                jnp.zeros((count * RHS, RANK), F32),
                jnp.zeros((count * RHS, 2 * RANK), F32),
            )

        def take_group(g, sofar):
            first = (GROUPS - 1 - g) * (group // 2)
            return take(
                recv, parent_w, parent_slots, LEAVES, PARENTS, first, group // 2, sofar
            )

        def take_whole_group(g, sofar):
            arrived = recv.at[n, pl.ds(devices - 1 - (g + 1) * group, group)]
            wait_for(arrived, recv_sem.at[n, g])
            return take_group(g, sofar)

        parent_sum = lax.fori_loop(0, GROUPS - 1, take_whole_group, nothing(PARENTS))
        wait_for(recv.at[n, pl.ds(0, group - 1)], recv_sem.at[n, GROUPS - 1])
        parent_sum = take_group(GROUPS - 1, parent_sum)
        wait_for(leaf_recv.at[n, pl.ds(0, CLOSE - 1)], recv_sem.at[n, GROUPS])
        leaf_sum = take(
            leaf_recv,
            leaf_w,
            leaf_slots,
            0,
            LEAVES,
            0,
            (CLOSE + 1) // 2,
            nothing(LEAVES),
        )

        def whole(through, handed):
            return through + (handed + swap_halves(handed))[:, :RANK]

        parent_far = whole(*parent_sum)
        leaf_far = whole(*leaf_sum)

        near_copy(n).wait_recv()
        total = total + near_in[n].astype(F32)
        for l in range(LEAVES):
            q = l // 2
            both = jnp.concatenate(
                [parent_far[q * RHS : (q + 1) * RHS], leaf_far[l * RHS : (l + 1) * RHS]], axis=1
            ).astype(BF16)
            value = total[l * RHS : (l + 1) * RHS] + nn(both, both_basis[l])
            value = value * point_mask[l]
            vector[l] = value
            out[n, l] = value
        out_copy(n).start()
        return carry

    lax.fori_loop(0, PRODUCTS, product, 0)

    def finish(n, carry):
        wait_for(send.at[n, pl.ds(0, devices - 1)], send_sem.at[n, 0])
        wait_for(leaf_send.at[n, pl.ds(0, CLOSE - 1)], send_sem.at[n, 1])
        x_copy(n).wait_send()
        near_copy(n).wait_send()
        out_copy(n).wait()
        return carry

    lax.fori_loop(0, PRODUCTS, finish, 0)


def on_device(
    start_vector,
    leaf_size,
    diag_blocks,
    near_blocks,
    near_count,
    near_first,
    near_second,
    leaf_basis,
    transfer,
    coupling,
    send_slot,
    far_target,
):
    devices = lax.axis_size("clu")
    tile = (RHS, 2 * RANK)
    close_pairs = (CLOSE + 1) // 2
    smem = pl.BlockSpec(memory_space=pltpu.SMEM)
    hbm = pl.BlockSpec(memory_space=pltpu.HBM)
    sides = (PRODUCTS, LEAVES * RHS, POINTS)
    return pl.pallas_call(
        functools.partial(kernel, devices),
        out_shape=jax.ShapeDtypeStruct((PRODUCTS, LEAVES, RHS, POINTS), F32),
        in_specs=[
            hbm,
            smem,
            hbm,
            hbm,
            smem,
            smem,
            smem,
            hbm,
            hbm,
            hbm,
            smem,
            smem,
        ],
        out_specs=hbm,
        scratch_shapes=[
            pltpu.VMEM((LEAVES, RHS, POINTS), F32),
            pltpu.VMEM((LEAVES, RANK, POINTS), BF16),
            pltpu.VMEM((LEAVES, RANK, RANK), F32),
            pltpu.VMEM((RANK, RANK, 2 * devices), F32),
            pltpu.VMEM((2 * devices * HALF, 2 * RANK), F32),
            pltpu.VMEM((devices // 2, RANK, 2 * RANK), BF16),
            pltpu.VMEM((close_pairs, RANK, 2 * RANK), BF16),
            pltpu.VMEM((devices // 2, 3, *tile), jnp.int32),
            pltpu.VMEM((close_pairs, 3, *tile), jnp.int32),
            pltpu.VMEM((CAPACITY, POINTS, POINTS), BF16),
            pltpu.VMEM((LEAVES, POINTS, POINTS), BF16),
            pltpu.VMEM((LEAVES, 2 * RANK, POINTS), BF16),
            pltpu.SMEM((CAPACITY, 3 * LEAVES), F32),
            pltpu.VMEM((LEAVES, RHS, POINTS), F32),
            pltpu.VMEM((LEAVES, RHS, POINTS), F32),
            pltpu.VMEM((PRODUCTS, LEAVES, RHS, POINTS), F32),
            pltpu.VMEM((2 * LEAVES, RHS, POINTS), F32),
            pltpu.VMEM((PRODUCTS, devices, *tile), BF16),
            pltpu.VMEM((PRODUCTS, devices, *tile), BF16),
            pltpu.VMEM((PRODUCTS, CLOSE + 1, *tile), BF16),
            pltpu.VMEM((PRODUCTS, CLOSE + 1, *tile), BF16),
            pltpu.VMEM(sides, BF16),
            pltpu.VMEM(sides, BF16),
            pltpu.VMEM(sides, BF16),
            pltpu.VMEM(sides, BF16),
            pltpu.SemaphoreType.DMA((LOADS + 3, 2)),
            pltpu.SemaphoreType.DMA((PRODUCTS,)),
            pltpu.SemaphoreType.DMA((PRODUCTS, 2)),
            pltpu.SemaphoreType.DMA((PRODUCTS, GROUPS + 1)),
            pltpu.SemaphoreType.DMA((PRODUCTS, 4)),
        ],
        compiler_params=pltpu.CompilerParams(
            collective_id=0, has_side_effects=True, vmem_limit_bytes=56 * 1024 * 1024
        ),
        name="h2_products",
    )(
        start_vector,
        leaf_size,
        diag_blocks,
        near_blocks,
        near_count,
        near_first,
        near_second,
        leaf_basis,
        transfer,
        coupling.transpose(1, 2, 0),
        send_slot,
        far_target,
    )


def solution(mesh):
    in_specs = (
        P("clu", None, None),
        P("clu"),
        P("clu", None, None),
        P("clu", None, None),
        P("clu"),
        P("clu"),
        P("clu"),
        P("clu", None, None),
        P("clu", None, None),
        P("clu", None, None),
        P("clu", None),
        P("clu", None),
    )
    out_specs = P(None, "clu", None, None)
    return jax.shard_map(
        on_device, mesh=mesh, in_specs=in_specs, out_specs=out_specs, check_vma=False
    )
```

time: 62.1 us -> 52.8 us (0.85)
  Pallas kernels: 59.7 us -> 50.4 us
    pallas_call x1, Pallas kernels: 59.7 us -> 50.4 us  [on_device(): pl.pallas_call(functools.partial(kernel, devices), out_shape=jax.ShapeDty...]
where the time goes in v7:
time: 52.8 us; the launch traced here: 52.7 us
  Pallas kernels  50.4 us (95%)
  local copies, waits for them, and re-layouts  1.57 us (3%)
  between operations  0.66 us (1%)
    pallas_call x1, Pallas kernels, on_device(): pl.pallas_call(functools.partial(kernel, devices), out_shape=jax.ShapeDty...  50.4 us
    unnamed x1, local copies, waits for them, and re-layouts  1.57 us

profile of v7, /device:TPU:1, one launch (start us, length us, event | category | flops | bytes accessed | tf_op | source)
XLA Modules:
  0.0 52.7 jit_solution(13125498812496578632)
XLA Ops:
  0.7 50.4 %h2_products.1 = f32[4,4,8,256]{3,2,1,0:T(8,128)} custom-call(f32[4,8,256]{2,1,0:T(8,128)} %start_hbm.1, s32[4]{0:T(128)} %leaf_size.1, bf16[4,256,256]{2,1,0:T(8,128)(2,1)} %diag_hbm.1, bf16[16,256,256]{2,1,0:T(8,128)(2,1)} %near_hbm.1, s32[1]{0:T(128)S(6)} %copy.14.near_count, s32[16]{0:T(128)} %near_first.1, s32[16]{0:T(128)} %near_second.1, ...), custom_call_target="tpu_custom_call" | custom-call | tf_op jit(solution)/shard_map/h2_products/pallas_call | solution.py:486
  51.1 1.6 %copy.15 = f32[4,4,8,256]{3,2,1,0:T(8,128)} copy(f32[4,4,8,256]{3,2,1,0:T(8,128)} %h2_products.1) | data formatting | bytes 262144

commit v8 on v7

--- a/solution.py
+++ b/solution.py
@@ -9,9 +9,10 @@
 
 PRODUCTS = 4
 REACH = 8
+LEAF_ROWS = 32
 CLOSE = 2 * REACH + 1
 GROUPS = 4
-STEP = 37
+GREETINGS = 7
 LOADS = 4
 LEAVES = 4
 PARENTS = LEAVES // 2
@@ -69,7 +70,6 @@
     near,
     diag,
     both_basis,
-    pick,
     point_mask,
     vector,
     out,
@@ -98,8 +98,11 @@
             return lax.rem(index, devices)
         return index & (devices - 1)
 
+    def flipped(index, w):
+        return index + w - 2 * (index & w)
+
     def partner(w):
-        return wrap(me + STEP * (w + 1))
+        return flipped(me, w)
 
     def leaf_partner(v):
         return wrap(me + (v - REACH + devices))
@@ -132,13 +135,19 @@
 
     barrier = pltpu.get_barrier_semaphore()
 
-    def greet(step, carry):
+    def greet(w):
         pl.semaphore_signal(
-            barrier, inc=1, device_id=(wrap(me + step),), device_id_type=MESH
-        )
+            barrier, inc=1, device_id=(partner(w),), device_id_type=MESH
+        )
+
+    def greet_some(k, carry):
+        for i in range(GREETINGS):
+            greet(1 + k * GREETINGS + i)
         return carry
 
-    lax.fori_loop(1, devices, greet, 0)
+    lax.fori_loop(0, (devices - 1) // GREETINGS, greet_some, 0)
+    for w in range(1 + (devices - 1) // GREETINGS * GREETINGS, devices):
+        greet(w)
 
     for load in small_loads:
         load.wait()
@@ -158,15 +167,22 @@
             [nn(high, own) + nn(low, own), own.astype(F32)], axis=0
         ).astype(BF16)
 
+    def one_hot(rows, wanted):
+        row = lax.broadcasted_iota(jnp.int32, (rows, pair_count), 0)
+        column = lax.broadcasted_iota(jnp.int32, (rows, pair_count), 1)
+        return jnp.where(column == wanted(row), 1.0, 0.0)
+
+    needed = jnp.concatenate(
+        [
+            one_hot(devices, lambda w: 2 * flipped(me, w) + 1),
+            one_hot(LEAF_ROWS, lambda v: 2 * leaf_partner(v)),
+        ],
+        axis=0,
+    ).astype(BF16)
+
     def turn(k, carry):
-        both = jnp.concatenate([raw[k], raw[k + HALF]], axis=0)
-        turned[pl.ds(k, pair_count, stride=HALF), :] = both.T
-        e = k // 2
-        live = e < near_count[0]
-        for i in range(6):
-            column = 6 * (k % 2) + i
-            leaf = jnp.where(column < LEAVES, near_first[e], near_second[e] + LEAVES)
-            pick[e, column] = jnp.where(live & (leaf == column), 1.0, 0.0)
+        both = jnp.concatenate([raw[k], raw[k + HALF]], axis=0).astype(BF16)
+        turned[pl.ds(k, devices + LEAF_ROWS, stride=HALF), :] = nt(needed, both)
         return carry
 
     for c in range(LOADS):
@@ -179,10 +195,9 @@
     def on_left(rows):
         return jnp.concatenate([left] * (rows // RHS), axis=0)
 
-    def build(w, slots, u, first, second):
+    def build(w, slots, u, row, first, second):
         tiles = [
-            turned[pl.ds(pl.multiple_of(column * HALF, HALF), HALF), :]
-            for column in (first, second)
+            turned[pl.ds(pl.multiple_of((row + i) * HALF, HALF), HALF), :] for i in range(2)
         ]
         swapped = [swap_halves(tile) for tile in tiles]
         w[u] = jnp.concatenate(
@@ -197,13 +212,13 @@
         slots[u, 2] = jnp.where(left, send_slot[0, second], send_slot[0, first])
 
     def build_parent(u, carry):
-        build(
-            parent_w, parent_slots, u, 2 * partner(2 * u) + 1, 2 * partner(2 * u + 1) + 1
-        )
+        first, second = [2 * partner(2 * u + i) + 1 for i in range(2)]
+        build(parent_w, parent_slots, u, 2 * u, first, second)
         return carry
 
     def build_leaf(u, carry):
-        build(leaf_w, leaf_slots, u, 2 * leaf_partner(2 * u), 2 * leaf_partner(2 * u + 1))
+        first, second = [2 * leaf_partner(2 * u + i) for i in range(2)]
+        build(leaf_w, leaf_slots, u, devices + 2 * u, first, second)
         return carry
 
     lax.fori_loop(0, devices // 2, build_parent, 0, unroll=8)
@@ -238,11 +253,10 @@
     def out_copy(n):
         return pltpu.make_async_copy(out.at[n], out_hbm.at[n], out_sem.at[n])
 
-    def parent_copy(n, g, i):
-        w = g * group + i
+    def parent_copy(n, w, g):
         return remote(
             send.at[n, pl.ds(w, 1)],
-            recv.at[n, pl.ds(devices - 2 - w, 1)],
+            recv.at[n, pl.ds(w, 1)],
             send_sem.at[n, 0],
             recv_sem.at[n, g],
             partner(w),
@@ -274,6 +288,13 @@
 
     def twos(first, count):
         return [[first + i for i in range(k, min(k + 2, count))] for k in range(0, count, 2)]
+
+    def hops(u):
+        return sum((0, 1, 2, 1)[u >> shift & 3] for shift in (0, 2, 4))
+
+    chips = devices // 2
+    order = sorted(range(1, chips), key=lambda u: (-hops(u), u * 37 % chips)) + [0]
+    chip_groups = [order[g * chips // GROUPS : (g + 1) * chips // GROUPS] for g in range(GROUPS)]
 
     def product(n, carry):
         exact = [vector[l] for l in range(LEAVES)]
@@ -303,10 +324,7 @@
                     store(2 * u + 1, jnp.where(left, outward, own).astype(BF16))
 
         def store_parent(w, tile):
-            if isinstance(w, int) and w == devices - 1:
-                recv[n, w] = tile
-            else:
-                send[n, w] = tile
+            send[n, w] = tile
 
         def store_leaf(v, tile):
             if v == REACH:
@@ -314,7 +332,7 @@
             elif v < CLOSE:
                 leaf_send[n, v] = tile
 
-        def send_group(g, count):
+        def fill_group(g, carry):
             fill(
                 parent_rows,
                 parent_twice,
@@ -325,15 +343,14 @@
                 group // 2,
                 store_parent,
             )
-            for i in range(count):
-                parent_copy(n, g, i).start()
-
-        def send_whole_group(g, carry):
-            send_group(g, group)
             return carry
 
-        lax.fori_loop(0, GROUPS - 1, send_whole_group, 0)
-        send_group(GROUPS - 1, group - 1)
+        lax.fori_loop(0, GROUPS, fill_group, 0)
+        for g in range(GROUPS):
+            for u in chip_groups[g]:
+                for w in (2 * u, 2 * u + 1):
+                    if w:
+                        parent_copy(n, w, g).start()
         fill(
             leaf_rows, leaf_twice, leaf_w, leaf_slots, 0, 0, (CLOSE + 1) // 2, store_leaf
         )
@@ -343,13 +360,18 @@
 
         for l in range(LEAVES):
             extended[l] = rounded[l].astype(F32)
+
+        def live_slot(slots, e):
+            slot = jnp.where(e < near_count[0], slots[e], -1)
+            return jnp.full((RHS, POINTS), slot, jnp.int32)
 
         def add_backward(step, sofar):
             for i in range(STRIDE):
                 e = step * STRIDE + i
                 own = extended[near_first[e]]
+                slot = live_slot(near_second, e)
                 spread = jnp.concatenate(
-                    [own * pick[e, LEAVES + s] for s in range(2 * LEAVES)], axis=0
+                    [jnp.where(slot == s, own, 0.0) for s in range(2 * LEAVES)], axis=0
                 ).astype(BF16)
                 sofar = sofar + nn(spread, near[e])
             return sofar
@@ -375,20 +397,23 @@
             for i in range(STRIDE):
                 e = step * STRIDE + i
                 other = extended[near_second[e]]
+                slot = live_slot(near_first, e)
                 spread = jnp.concatenate(
-                    [other * pick[e, t] for t in range(LEAVES)], axis=0
+                    [jnp.where(slot == t, other, 0.0) for t in range(LEAVES)], axis=0
                 ).astype(BF16)
                 sofar = sofar + nt(spread, near[e])
             return sofar
 
         total = lax.fori_loop(0, CAPACITY // STRIDE, add_forward, total)
 
-        def take(box, w, slots, first_slot, slot_count, first, count, sofar):
+        def take(box, w, slots, first_slot, slot_count, pairs, sofar):
             through, handed = sofar
-            for us in twos(first, count):
-                rows = []
+            for k in range(0, len(pairs), 2):
+                us, rows = pairs[k : k + 2], []
                 for u in us:
-                    even, odd = box[n, 2 * u].astype(F32), box[n, 2 * u + 1].astype(F32)
+                    outer = send if u == 0 and box is recv else box
+                    even = outer[n, 2 * u].astype(F32)
+                    odd = box[n, 2 * u + 1].astype(F32)
                     incoming = jnp.where(left, even, odd)
                     outcome = jnp.where(left, odd, even)
                     rows.append(kept(slots[u, 0], incoming, first_slot, slot_count))
@@ -404,20 +429,13 @@
                 jnp.zeros((count * RHS, 2 * RANK), F32),
             )
 
-        def take_group(g, sofar):
-            first = (GROUPS - 1 - g) * (group // 2)
-            return take(
-                recv, parent_w, parent_slots, LEAVES, PARENTS, first, group // 2, sofar
+        parent_sum = nothing(PARENTS)
+        for g in range(GROUPS):
+            messages = group if g < GROUPS - 1 else group - 1
+            wait_for(recv.at[n, pl.ds(1, messages)], recv_sem.at[n, g])
+            parent_sum = take(
+                recv, parent_w, parent_slots, LEAVES, PARENTS, chip_groups[g], parent_sum
             )
-
-        def take_whole_group(g, sofar):
-            arrived = recv.at[n, pl.ds(devices - 1 - (g + 1) * group, group)]
-            wait_for(arrived, recv_sem.at[n, g])
-            return take_group(g, sofar)
-
-        parent_sum = lax.fori_loop(0, GROUPS - 1, take_whole_group, nothing(PARENTS))
-        wait_for(recv.at[n, pl.ds(0, group - 1)], recv_sem.at[n, GROUPS - 1])
-        parent_sum = take_group(GROUPS - 1, parent_sum)
         wait_for(leaf_recv.at[n, pl.ds(0, CLOSE - 1)], recv_sem.at[n, GROUPS])
         leaf_sum = take(
             leaf_recv,
@@ -425,8 +443,7 @@
             leaf_slots,
             0,
             LEAVES,
-            0,
-            (CLOSE + 1) // 2,
+            list(range((CLOSE + 1) // 2)),
             nothing(LEAVES),
         )
 
@@ -453,7 +470,7 @@
     lax.fori_loop(0, PRODUCTS, product, 0)
 
     def finish(n, carry):
-        wait_for(send.at[n, pl.ds(0, devices - 1)], send_sem.at[n, 0])
+        wait_for(send.at[n, pl.ds(1, devices - 1)], send_sem.at[n, 0])
         wait_for(leaf_send.at[n, pl.ds(0, CLOSE - 1)], send_sem.at[n, 1])
         x_copy(n).wait_send()
         near_copy(n).wait_send()
@@ -506,7 +523,7 @@
             pltpu.VMEM((LEAVES, RANK, POINTS), BF16),
             pltpu.VMEM((LEAVES, RANK, RANK), F32),
             pltpu.VMEM((RANK, RANK, 2 * devices), F32),
-            pltpu.VMEM((2 * devices * HALF, 2 * RANK), F32),
+            pltpu.VMEM(((devices + LEAF_ROWS) * HALF, 2 * RANK), F32),
             pltpu.VMEM((devices // 2, RANK, 2 * RANK), BF16),
             pltpu.VMEM((close_pairs, RANK, 2 * RANK), BF16),
             pltpu.VMEM((devices // 2, 3, *tile), jnp.int32),
@@ -514,7 +531,6 @@
             pltpu.VMEM((CAPACITY, POINTS, POINTS), BF16),
             pltpu.VMEM((LEAVES, POINTS, POINTS), BF16),
             pltpu.VMEM((LEAVES, 2 * RANK, POINTS), BF16),
-            pltpu.SMEM((CAPACITY, 3 * LEAVES), F32),
             pltpu.VMEM((LEAVES, RHS, POINTS), F32),
             pltpu.VMEM((LEAVES, RHS, POINTS), F32),
             pltpu.VMEM((PRODUCTS, LEAVES, RHS, POINTS), F32),

time: 52.8 us -> 52.6 us (level)
  no operation moved by 1% of the time
where the time goes in v8:
time: 52.6 us; the launch traced here: 52.5 us
  Pallas kernels  50.2 us (95%)
  local copies, waits for them, and re-layouts  1.57 us (3%)
  between operations  0.66 us (1%)
    pallas_call x1, Pallas kernels, on_device(): pl.pallas_call(functools.partial(kernel, devices), out_shape=jax.ShapeDty...  50.2 us
    unnamed x1, local copies, waits for them, and re-layouts  1.57 us

profile of v8, /device:TPU:1, one launch (start us, length us, event | category | flops | bytes accessed | tf_op | source)
XLA Modules:
  0.0 52.5 jit_solution(5816205735053006307)
XLA Ops:
  0.7 50.2 %h2_products.1 = f32[4,4,8,256]{3,2,1,0:T(8,128)} custom-call(f32[4,8,256]{2,1,0:T(8,128)} %start_hbm.1, s32[4]{0:T(128)} %leaf_size.1, bf16[4,256,256]{2,1,0:T(8,128)(2,1)} %diag_hbm.1, bf16[16,256,256]{2,1,0:T(8,128)(2,1)} %near_hbm.1, s32[1]{0:T(128)S(6)} %copy.14.near_count, s32[16]{0:T(128)} %near_first.1, s32[16]{0:T(128)} %near_second.1, ...), custom_call_target="tpu_custom_call" | custom-call | tf_op jit(solution)/shard_map/h2_products/pallas_call | solution.py:503
  50.9 1.6 %copy.15 = f32[4,4,8,256]{3,2,1,0:T(8,128)} copy(f32[4,4,8,256]{3,2,1,0:T(8,128)} %h2_products.1) | data formatting | bytes 262144

commit v9 on v8

--- a/solution.py
+++ b/solution.py
@@ -21,7 +21,7 @@
 RHS = 8
 POINTS = 256
 CAPACITY = 16
-STRIDE = 4
+STRIDE = 8
 MESH = pl.DeviceIdType.MESH
 F32 = jnp.float32
 BF16 = jnp.bfloat16
@@ -70,6 +70,9 @@
     near,
     diag,
     both_basis,
+    gram,
+    coefs,
+    last_far,
     point_mask,
     vector,
     out,
@@ -166,6 +169,10 @@
         both_basis[l] = jnp.concatenate(
             [nn(high, own) + nn(low, own), own.astype(F32)], axis=0
         ).astype(BF16)
+        masked = both_basis[l].astype(F32) * point_mask[l][:1]
+        gram[l] = nt(masked.astype(BF16), both_basis[l]).astype(BF16)
+        coefs[l] = nt(vector[l].astype(BF16), both_basis[l])
+        last_far[l] = jnp.zeros((RHS, 2 * RANK), F32)
 
     def one_hot(rows, wanted):
         row = lax.broadcasted_iota(jnp.int32, (rows, pair_count), 0)
@@ -251,7 +258,7 @@
         )
 
     def out_copy(n):
-        return pltpu.make_async_copy(out.at[n], out_hbm.at[n], out_sem.at[n])
+        return pltpu.make_async_copy(out.at[n + 1], out_hbm.at[n], out_sem.at[n])
 
     def parent_copy(n, w, g):
         return remote(
@@ -286,23 +293,27 @@
             [jnp.where(slot == first + t, value, 0.0) for t in range(count)], axis=0
         )
 
-    def twos(first, count):
-        return [[first + i for i in range(k, min(k + 2, count))] for k in range(0, count, 2)]
-
     def hops(u):
         return sum((0, 1, 2, 1)[u >> shift & 3] for shift in (0, 2, 4))
 
     chips = devices // 2
     order = sorted(range(1, chips), key=lambda u: (-hops(u), u * 37 % chips)) + [0]
-    chip_groups = [order[g * chips // GROUPS : (g + 1) * chips // GROUPS] for g in range(GROUPS)]
+    leaf_pairs = list(range((CLOSE + 1) // 2))
+    cuts = [0, chips // 8, 3 * chips // 8, 11 * chips // 16, chips]
+    chip_groups = [order[cuts[g] : cuts[g + 1]] for g in range(GROUPS)]
+
+    def finish_vector(n):
+        values = []
+        for l in range(LEAVES):
+            value = vector[l] + nn(last_far[l].astype(BF16), both_basis[l])
+            value = value * point_mask[l]
+            out[n, l] = value
+            values.append(value)
+        return values
 
     def product(n, carry):
-        exact = [vector[l] for l in range(LEAVES)]
-        rounded = [value.astype(BF16) for value in exact]
-        x_out[n] = jnp.concatenate(exact, axis=0).astype(BF16)
-        x_copy(n).start()
-
-        coef = [nt(rounded[l], both_basis[l]) for l in range(LEAVES)]
+        coef = [coefs[l] for l in range(LEAVES)]
+
         parent = jnp.concatenate(
             [coef[2 * q] + coef[2 * q + 1] for q in range(PARENTS)], axis=0
         )
@@ -313,8 +324,9 @@
         parent_rows = parent[:, :RANK].astype(BF16)
         leaf_rows = leaf_turned[:, :RANK].astype(BF16)
 
-        def fill(rows, twice, w, slots, first_slot, first, count, store):
-            for us in twos(first, count):
+        def fill(rows, twice, w, slots, first_slot, pairs, store):
+            for k in range(0, len(pairs), 2):
+                us = pairs[k : k + 2]
                 made = nn(rows, side_by_side([w[u] for u in us]))
                 for i, u in enumerate(us):
                     block = made[:, i * 2 * RANK : (i + 1) * 2 * RANK]
@@ -332,31 +344,35 @@
             elif v < CLOSE:
                 leaf_send[n, v] = tile
 
-        def fill_group(g, carry):
+        for g in range(GROUPS):
             fill(
                 parent_rows,
                 parent_twice,
                 parent_w,
                 parent_slots,
                 LEAVES,
-                g * (group // 2),
-                group // 2,
+                chip_groups[g],
                 store_parent,
             )
-            return carry
-
-        lax.fori_loop(0, GROUPS, fill_group, 0)
-        for g in range(GROUPS):
             for u in chip_groups[g]:
                 for w in (2 * u, 2 * u + 1):
                     if w:
                         parent_copy(n, w, g).start()
         fill(
-            leaf_rows, leaf_twice, leaf_w, leaf_slots, 0, 0, (CLOSE + 1) // 2, store_leaf
+            leaf_rows, leaf_twice, leaf_w, leaf_slots, 0, leaf_pairs, store_leaf
         )
         for v in range(CLOSE):
             if v != REACH:
                 leaf_copy(n, v).start()
+
+        exact = finish_vector(n)
+        rounded = [value.astype(BF16) for value in exact]
+        x_out[n] = jnp.concatenate(exact, axis=0).astype(BF16)
+        x_copy(n).start()
+
+        @pl.when(n > 0)
+        def _():
+            out_copy(n - 1).start()
 
         for l in range(LEAVES):
             extended[l] = rounded[l].astype(F32)
@@ -429,22 +445,25 @@
                 jnp.zeros((count * RHS, 2 * RANK), F32),
             )
 
+        near_copy(n).wait_recv()
+        total = total + near_in[n].astype(F32)
+        near_coef = []
+        for l in range(LEAVES):
+            value = total[l * RHS : (l + 1) * RHS] * point_mask[l]
+            vector[l] = value
+            near_coef.append(nt(value.astype(BF16), both_basis[l]))
+
         parent_sum = nothing(PARENTS)
         for g in range(GROUPS):
-            messages = group if g < GROUPS - 1 else group - 1
+            messages = 2 * len(chip_groups[g]) - (1 if g == GROUPS - 1 else 0)
             wait_for(recv.at[n, pl.ds(1, messages)], recv_sem.at[n, g])
+            if g == GROUPS - 1:
+                wait_for(leaf_recv.at[n, pl.ds(0, CLOSE - 1)], recv_sem.at[n, GROUPS])
             parent_sum = take(
                 recv, parent_w, parent_slots, LEAVES, PARENTS, chip_groups[g], parent_sum
             )
-        wait_for(leaf_recv.at[n, pl.ds(0, CLOSE - 1)], recv_sem.at[n, GROUPS])
         leaf_sum = take(
-            leaf_recv,
-            leaf_w,
-            leaf_slots,
-            0,
-            LEAVES,
-            list(range((CLOSE + 1) // 2)),
-            nothing(LEAVES),
+            leaf_recv, leaf_w, leaf_slots, 0, LEAVES, leaf_pairs, nothing(LEAVES)
         )
 
         def whole(through, handed):
@@ -453,21 +472,18 @@
         parent_far = whole(*parent_sum)
         leaf_far = whole(*leaf_sum)
 
-        near_copy(n).wait_recv()
-        total = total + near_in[n].astype(F32)
         for l in range(LEAVES):
             q = l // 2
             both = jnp.concatenate(
                 [parent_far[q * RHS : (q + 1) * RHS], leaf_far[l * RHS : (l + 1) * RHS]], axis=1
-            ).astype(BF16)
-            value = total[l * RHS : (l + 1) * RHS] + nn(both, both_basis[l])
-            value = value * point_mask[l]
-            vector[l] = value
-            out[n, l] = value
-        out_copy(n).start()
+            )
+            last_far[l] = both
+            coefs[l] = near_coef[l] + nn(both.astype(BF16), gram[l])
         return carry
 
     lax.fori_loop(0, PRODUCTS, product, 0)
+    finish_vector(PRODUCTS)
+    out_copy(PRODUCTS - 1).start()
 
     def finish(n, carry):
         wait_for(send.at[n, pl.ds(1, devices - 1)], send_sem.at[n, 0])
@@ -531,9 +547,12 @@
             pltpu.VMEM((CAPACITY, POINTS, POINTS), BF16),
             pltpu.VMEM((LEAVES, POINTS, POINTS), BF16),
             pltpu.VMEM((LEAVES, 2 * RANK, POINTS), BF16),
+            pltpu.VMEM((LEAVES, 2 * RANK, 2 * RANK), BF16),
+            pltpu.VMEM((LEAVES, *tile), F32),
+            pltpu.VMEM((LEAVES, *tile), F32),
             pltpu.VMEM((LEAVES, RHS, POINTS), F32),
             pltpu.VMEM((LEAVES, RHS, POINTS), F32),
-            pltpu.VMEM((PRODUCTS, LEAVES, RHS, POINTS), F32),
+            pltpu.VMEM((PRODUCTS + 1, LEAVES, RHS, POINTS), F32),
             pltpu.VMEM((2 * LEAVES, RHS, POINTS), F32),
             pltpu.VMEM((PRODUCTS, devices, *tile), BF16),
             pltpu.VMEM((PRODUCTS, devices, *tile), BF16),

time: 52.6 us -> 51.9 us (0.987)
  Pallas kernels: 50.2 us -> 49 us
    pallas_call x1, Pallas kernels: 50.2 us -> 49 us  [on_device(): pl.pallas_call(functools.partial(kernel, devices), out_shape=jax.ShapeDty...]
where the time goes in v9:
time: 51.9 us; the launch traced here: 51.3 us
  Pallas kernels  49 us (94%)
  local copies, waits for them, and re-layouts  1.57 us (3%)
  between operations  0.66 us (1%)
    pallas_call x1, Pallas kernels, on_device(): pl.pallas_call(functools.partial(kernel, devices), out_shape=jax.ShapeDty...  49 us
    unnamed x1, local copies, waits for them, and re-layouts  1.57 us

profile of v9, /device:TPU:1, one launch (start us, length us, event | category | flops | bytes accessed | tf_op | source)
XLA Modules:
  0.0 51.3 jit_solution(9211232775019797184)
XLA Ops:
  0.7 49.0 %h2_products.1 = f32[4,4,8,256]{3,2,1,0:T(8,128)} custom-call(f32[4,8,256]{2,1,0:T(8,128)} %start_hbm.1, s32[4]{0:T(128)} %leaf_size.1, bf16[4,256,256]{2,1,0:T(8,128)(2,1)} %diag_hbm.1, bf16[16,256,256]{2,1,0:T(8,128)(2,1)} %near_hbm.1, s32[1]{0:T(128)S(6)} %copy.14.near_count, s32[16]{0:T(128)} %near_first.1, s32[16]{0:T(128)} %near_second.1, ...), custom_call_target="tpu_custom_call" | custom-call | tf_op jit(solution)/shard_map/h2_products/pallas_call | solution.py:519
  49.7 1.6 %copy.15 = f32[4,4,8,256]{3,2,1,0:T(8,128)} copy(f32[4,4,8,256]{3,2,1,0:T(8,128)} %h2_products.1) | data formatting | bytes 262144

commit v10 on v9

--- a/solution.py
+++ b/solution.py
@@ -77,6 +77,7 @@
     vector,
     out,
     extended,
+    hand,
     send,
     recv,
     leaf_send,
@@ -87,12 +88,15 @@
     near_in,
     load_sem,
     out_sem,
+    hand_sem,
+    handed_sem,
     send_sem,
     recv_sem,
     side_sem,
 ):
     me = lax.axis_index("clu")
-    group = devices // GROUPS
+    chips = devices // 2
+    group = chips // GROUPS
     load_rows = HALF // LOADS
     pair_count = 2 * devices
 
@@ -104,8 +108,11 @@
     def flipped(index, w):
         return index + w - 2 * (index & w)
 
+    def mixed(w):
+        return flipped(w, 4 * (w & 24) & (devices - 1))
+
     def partner(w):
-        return flipped(me, w)
+        return flipped(me, mixed(w))
 
     def leaf_partner(v):
         return wrap(me + (v - REACH + devices))
@@ -181,7 +188,7 @@
 
     needed = jnp.concatenate(
         [
-            one_hot(devices, lambda w: 2 * flipped(me, w) + 1),
+            one_hot(devices, lambda w: 2 * partner(w) + 1),
             one_hot(LEAF_ROWS, lambda v: 2 * leaf_partner(v)),
         ],
         axis=0,
@@ -260,13 +267,23 @@
     def out_copy(n):
         return pltpu.make_async_copy(out.at[n + 1], out_hbm.at[n], out_sem.at[n])
 
-    def parent_copy(n, w, g):
+    def hand_copy(n, g):
+        chips_of = pl.ds(g * group, group)
         return remote(
-            send.at[n, pl.ds(w, 1)],
-            recv.at[n, pl.ds(w, 1)],
+            hand.at[n, chips_of],
+            send.at[n, chips_of, 1],
+            hand_sem.at[n],
+            handed_sem.at[n, g],
+            partner(1),
+        )
+
+    def parent_copy(n, u, g):
+        return remote(
+            send.at[n, u],
+            recv.at[n, u],
             send_sem.at[n, 0],
             recv_sem.at[n, g],
-            partner(w),
+            partner(2 * u),
         )
 
     def leaf_copy(n, v):
@@ -294,13 +311,12 @@
         )
 
     def hops(u):
-        return sum((0, 1, 2, 1)[u >> shift & 3] for shift in (0, 2, 4))
-
-    chips = devices // 2
-    order = sorted(range(1, chips), key=lambda u: (-hops(u), u * 37 % chips)) + [0]
+        return sum((0, 1, 2, 1)[mixed(2 * u) >> shift & 3] for shift in (1, 3, 5))
+
+    def chips_in(g):
+        return list(range(g * group, (g + 1) * group))
+
     leaf_pairs = list(range((CLOSE + 1) // 2))
-    cuts = [0, chips // 8, 3 * chips // 8, 11 * chips // 16, chips]
-    chip_groups = [order[cuts[g] : cuts[g + 1]] for g in range(GROUPS)]
 
     def finish_vector(n):
         values = []
@@ -336,7 +352,10 @@
                     store(2 * u + 1, jnp.where(left, outward, own).astype(BF16))
 
         def store_parent(w, tile):
-            send[n, w] = tile
+            if w % 2:
+                hand[n, w // 2] = tile
+            else:
+                send[n, w // 2, 0] = tile
 
         def store_leaf(v, tile):
             if v == REACH:
@@ -344,20 +363,30 @@
             elif v < CLOSE:
                 leaf_send[n, v] = tile
 
-        for g in range(GROUPS):
+        def fill_group(g):
             fill(
                 parent_rows,
                 parent_twice,
                 parent_w,
                 parent_slots,
                 LEAVES,
-                chip_groups[g],
+                chips_in(g),
                 store_parent,
             )
-            for u in chip_groups[g]:
-                for w in (2 * u, 2 * u + 1):
-                    if w:
-                        parent_copy(n, w, g).start()
+            hand_copy(n, g).start()
+
+        def send_group(g):
+            wait_for(send.at[n, pl.ds(g * group, group), 1], handed_sem.at[n, g])
+            for u in sorted(chips_in(g), key=hops, reverse=True):
+                if u:
+                    parent_copy(n, u, g).start()
+
+        fill_group(1)
+        fill_group(2)
+        fill_group(3)
+        send_group(1)
+        fill_group(0)
+        send_group(2)
         fill(
             leaf_rows, leaf_twice, leaf_w, leaf_slots, 0, leaf_pairs, store_leaf
         )
@@ -365,10 +394,13 @@
             if v != REACH:
                 leaf_copy(n, v).start()
 
+        send_group(3)
         exact = finish_vector(n)
         rounded = [value.astype(BF16) for value in exact]
         x_out[n] = jnp.concatenate(exact, axis=0).astype(BF16)
         x_copy(n).start()
+
+        send_group(0)
 
         @pl.when(n > 0)
         def _():
@@ -422,14 +454,12 @@
 
         total = lax.fori_loop(0, CAPACITY // STRIDE, add_forward, total)
 
-        def take(box, w, slots, first_slot, slot_count, pairs, sofar):
+        def take(tiles, w, slots, first_slot, slot_count, pairs, sofar):
             through, handed = sofar
             for k in range(0, len(pairs), 2):
                 us, rows = pairs[k : k + 2], []
                 for u in us:
-                    outer = send if u == 0 and box is recv else box
-                    even = outer[n, 2 * u].astype(F32)
-                    odd = box[n, 2 * u + 1].astype(F32)
+                    even, odd = [tile.astype(F32) for tile in tiles(u)]
                     incoming = jnp.where(left, even, odd)
                     outcome = jnp.where(left, odd, even)
                     rows.append(kept(slots[u, 0], incoming, first_slot, slot_count))
@@ -453,17 +483,29 @@
             vector[l] = value
             near_coef.append(nt(value.astype(BF16), both_basis[l]))
 
-        parent_sum = nothing(PARENTS)
-        for g in range(GROUPS):
-            messages = 2 * len(chip_groups[g]) - (1 if g == GROUPS - 1 else 0)
-            wait_for(recv.at[n, pl.ds(1, messages)], recv_sem.at[n, g])
-            if g == GROUPS - 1:
-                wait_for(leaf_recv.at[n, pl.ds(0, CLOSE - 1)], recv_sem.at[n, GROUPS])
-            parent_sum = take(
-                recv, parent_w, parent_slots, LEAVES, PARENTS, chip_groups[g], parent_sum
+        def parent_tiles(u):
+            box = send if isinstance(u, int) and u == 0 else recv
+            return box[n, u, 0], box[n, u, 1]
+
+        def leaf_tiles(u):
+            return leaf_recv[n, 2 * u], leaf_recv[n, 2 * u + 1]
+
+        def take_group(g, sofar):
+            pairs = [g * group + i for i in range(group)]
+            return take(
+                parent_tiles, parent_w, parent_slots, LEAVES, PARENTS, pairs, sofar
             )
+
+        def take_whole_group(g, sofar):
+            wait_for(recv.at[n, pl.ds(g * group, group)], recv_sem.at[n, g])
+            return take_group(g, sofar)
+
+        parent_sum = lax.fori_loop(1, GROUPS, take_whole_group, nothing(PARENTS))
+        wait_for(recv.at[n, pl.ds(1, group - 1)], recv_sem.at[n, 0])
+        wait_for(leaf_recv.at[n, pl.ds(0, CLOSE - 1)], recv_sem.at[n, GROUPS])
+        parent_sum = take_group(0, parent_sum)
         leaf_sum = take(
-            leaf_recv, leaf_w, leaf_slots, 0, LEAVES, leaf_pairs, nothing(LEAVES)
+            leaf_tiles, leaf_w, leaf_slots, 0, LEAVES, leaf_pairs, nothing(LEAVES)
         )
 
         def whole(through, handed):
@@ -486,7 +528,8 @@
     out_copy(PRODUCTS - 1).start()
 
     def finish(n, carry):
-        wait_for(send.at[n, pl.ds(1, devices - 1)], send_sem.at[n, 0])
+        wait_for(hand.at[n], hand_sem.at[n])
+        wait_for(send.at[n, pl.ds(1, chips - 1)], send_sem.at[n, 0])
         wait_for(leaf_send.at[n, pl.ds(0, CLOSE - 1)], send_sem.at[n, 1])
         x_copy(n).wait_send()
         near_copy(n).wait_send()
@@ -554,8 +597,9 @@
             pltpu.VMEM((LEAVES, RHS, POINTS), F32),
             pltpu.VMEM((PRODUCTS + 1, LEAVES, RHS, POINTS), F32),
             pltpu.VMEM((2 * LEAVES, RHS, POINTS), F32),
-            pltpu.VMEM((PRODUCTS, devices, *tile), BF16),
-            pltpu.VMEM((PRODUCTS, devices, *tile), BF16),
+            pltpu.VMEM((PRODUCTS, devices // 2, *tile), BF16),
+            pltpu.VMEM((PRODUCTS, devices // 2, 2, *tile), BF16),
+            pltpu.VMEM((PRODUCTS, devices // 2, 2, *tile), BF16),
             pltpu.VMEM((PRODUCTS, CLOSE + 1, *tile), BF16),
             pltpu.VMEM((PRODUCTS, CLOSE + 1, *tile), BF16),
             pltpu.VMEM(sides, BF16),
@@ -564,6 +608,8 @@
             pltpu.VMEM(sides, BF16),
             pltpu.SemaphoreType.DMA((LOADS + 3, 2)),
             pltpu.SemaphoreType.DMA((PRODUCTS,)),
+            pltpu.SemaphoreType.DMA((PRODUCTS,)),
+            pltpu.SemaphoreType.DMA((PRODUCTS, GROUPS)),
             pltpu.SemaphoreType.DMA((PRODUCTS, 2)),
             pltpu.SemaphoreType.DMA((PRODUCTS, GROUPS + 1)),
             pltpu.SemaphoreType.DMA((PRODUCTS, 4)),

time: 51.9 us -> 55.9 us (1.077)
  Pallas kernels: 49 us -> 53.5 us
    pallas_call x1, Pallas kernels: 49 us -> 53.5 us  [on_device(): pl.pallas_call(functools.partial(kernel, devices), out_shape=jax.ShapeDty...]
where the time goes in v10:
time: 55.9 us; the launch traced here: 55.7 us
  Pallas kernels  53.5 us (96%)
  local copies, waits for them, and re-layouts  1.57 us (3%)
  between operations  0.66 us (1%)
    pallas_call x1, Pallas kernels, on_device(): pl.pallas_call(functools.partial(kernel, devices), out_shape=jax.ShapeDty...  53.5 us
    unnamed x1, local copies, waits for them, and re-layouts  1.57 us

profile of v10, /device:TPU:1, one launch (start us, length us, event | category | flops | bytes accessed | tf_op | source)
XLA Modules:
  0.0 55.7 jit_solution(3358174632762279668)
XLA Ops:
  0.7 53.5 %h2_products.1 = f32[4,4,8,256]{3,2,1,0:T(8,128)} custom-call(f32[4,8,256]{2,1,0:T(8,128)} %start_hbm.1, s32[4]{0:T(128)} %leaf_size.1, bf16[4,256,256]{2,1,0:T(8,128)(2,1)} %diag_hbm.1, bf16[16,256,256]{2,1,0:T(8,128)(2,1)} %near_hbm.1, s32[1]{0:T(128)S(6)} %copy.14.near_count, s32[16]{0:T(128)} %near_first.1, s32[16]{0:T(128)} %near_second.1, ...), custom_call_target="tpu_custom_call" | custom-call | tf_op jit(solution)/shard_map/h2_products/pallas_call | solution.py:562
  54.2 1.6 %copy.15 = f32[4,4,8,256]{3,2,1,0:T(8,128)} copy(f32[4,4,8,256]{3,2,1,0:T(8,128)} %h2_products.1) | data formatting | bytes 262144

commit v11 on v9

--- a/solution.py
+++ b/solution.py
@@ -454,17 +454,16 @@
             near_coef.append(nt(value.astype(BF16), both_basis[l]))
 
         parent_sum = nothing(PARENTS)
-        for g in range(GROUPS):
+        wait_for(leaf_recv.at[n, pl.ds(0, CLOSE - 1)], recv_sem.at[n, GROUPS])
+        leaf_sum = take(
+            leaf_recv, leaf_w, leaf_slots, 0, LEAVES, leaf_pairs, nothing(LEAVES)
+        )
+        for g in reversed(range(GROUPS)):
             messages = 2 * len(chip_groups[g]) - (1 if g == GROUPS - 1 else 0)
             wait_for(recv.at[n, pl.ds(1, messages)], recv_sem.at[n, g])
-            if g == GROUPS - 1:
-                wait_for(leaf_recv.at[n, pl.ds(0, CLOSE - 1)], recv_sem.at[n, GROUPS])
             parent_sum = take(
                 recv, parent_w, parent_slots, LEAVES, PARENTS, chip_groups[g], parent_sum
             )
-        leaf_sum = take(
-            leaf_recv, leaf_w, leaf_slots, 0, LEAVES, leaf_pairs, nothing(LEAVES)
-        )
 
         def whole(through, handed):
             return through + (handed + swap_halves(handed))[:, :RANK]

time: 51.9 us -> 52.7 us (1.015)
  Pallas kernels: 49 us -> 50.3 us
    pallas_call x1, Pallas kernels: 49 us -> 50.3 us  [on_device(): pl.pallas_call(functools.partial(kernel, devices), out_shape=jax.ShapeDty...]
where the time goes in v11:
time: 52.7 us; the launch traced here: 52.6 us
  Pallas kernels  50.3 us (95%)
  local copies, waits for them, and re-layouts  1.57 us (3%)
  between operations  0.66 us (1%)
    pallas_call x1, Pallas kernels, on_device(): pl.pallas_call(functools.partial(kernel, devices), out_shape=jax.ShapeDty...  50.3 us
    unnamed x1, local copies, waits for them, and re-layouts  1.57 us

profile of v11, /device:TPU:1, one launch (start us, length us, event | category | flops | bytes accessed | tf_op | source)
XLA Modules:
  0.0 52.6 jit_solution(214217422028635727)
XLA Ops:
  0.7 50.3 %h2_products.1 = f32[4,4,8,256]{3,2,1,0:T(8,128)} custom-call(f32[4,8,256]{2,1,0:T(8,128)} %start_hbm.1, s32[4]{0:T(128)} %leaf_size.1, bf16[4,256,256]{2,1,0:T(8,128)(2,1)} %diag_hbm.1, bf16[16,256,256]{2,1,0:T(8,128)(2,1)} %near_hbm.1, s32[1]{0:T(128)S(6)} %copy.14.near_count, s32[16]{0:T(128)} %near_first.1, s32[16]{0:T(128)} %near_second.1, ...), custom_call_target="tpu_custom_call" | custom-call | tf_op jit(solution)/shard_map/h2_products/pallas_call | solution.py:518
  51.0 1.6 %copy.15 = f32[4,4,8,256]{3,2,1,0:T(8,128)} copy(f32[4,4,8,256]{3,2,1,0:T(8,128)} %h2_products.1) | data formatting | bytes 262144

commit v12 on v9

--- a/solution.py
+++ b/solution.py
@@ -11,7 +11,8 @@
 REACH = 8
 LEAF_ROWS = 32
 CLOSE = 2 * REACH + 1
-GROUPS = 4
+CUTS = (0, 8, 16, 26, 38, 50, 64)
+GROUPS = len(CUTS) - 1
 GREETINGS = 7
 LOADS = 4
 LEAVES = 4
@@ -21,7 +22,7 @@
 RHS = 8
 POINTS = 256
 CAPACITY = 16
-STRIDE = 8
+STRIDE = 4
 MESH = pl.DeviceIdType.MESH
 F32 = jnp.float32
 BF16 = jnp.bfloat16
@@ -92,7 +93,6 @@
     side_sem,
 ):
     me = lax.axis_index("clu")
-    group = devices // GROUPS
     load_rows = HALF // LOADS
     pair_count = 2 * devices
 
@@ -299,7 +299,7 @@
     chips = devices // 2
     order = sorted(range(1, chips), key=lambda u: (-hops(u), u * 37 % chips)) + [0]
     leaf_pairs = list(range((CLOSE + 1) // 2))
-    cuts = [0, chips // 8, 3 * chips // 8, 11 * chips // 16, chips]
+    cuts = [cut * chips // CUTS[-1] for cut in CUTS]
     chip_groups = [order[cuts[g] : cuts[g + 1]] for g in range(GROUPS)]
 
     def finish_vector(n):
@@ -344,7 +344,7 @@
             elif v < CLOSE:
                 leaf_send[n, v] = tile
 
-        for g in range(GROUPS):
+        def fill_group(g):
             fill(
                 parent_rows,
                 parent_twice,
@@ -354,28 +354,12 @@
                 chip_groups[g],
                 store_parent,
             )
+
+        def send_group(g):
             for u in chip_groups[g]:
                 for w in (2 * u, 2 * u + 1):
                     if w:
                         parent_copy(n, w, g).start()
-        fill(
-            leaf_rows, leaf_twice, leaf_w, leaf_slots, 0, leaf_pairs, store_leaf
-        )
-        for v in range(CLOSE):
-            if v != REACH:
-                leaf_copy(n, v).start()
-
-        exact = finish_vector(n)
-        rounded = [value.astype(BF16) for value in exact]
-        x_out[n] = jnp.concatenate(exact, axis=0).astype(BF16)
-        x_copy(n).start()
-
-        @pl.when(n > 0)
-        def _():
-            out_copy(n - 1).start()
-
-        for l in range(LEAVES):
-            extended[l] = rounded[l].astype(F32)
 
         def live_slot(slots, e):
             slot = jnp.where(e < near_count[0], slots[e], -1)
@@ -392,23 +376,6 @@
                 sofar = sofar + nn(spread, near[e])
             return sofar
 
-        backward = lax.fori_loop(
-            0,
-            CAPACITY // STRIDE,
-            add_backward,
-            jnp.zeros((2 * LEAVES * RHS, POINTS), F32),
-        )
-        near_out[n] = backward[LEAVES * RHS :].astype(BF16)
-        near_copy(n).start()
-        total = backward[: LEAVES * RHS] + jnp.concatenate(
-            [nn(rounded[l], diag[l]) for l in range(LEAVES)], axis=0
-        )
-
-        x_copy(n).wait_recv()
-        following = x_in[n].astype(F32)
-        for l in range(LEAVES):
-            extended[LEAVES + l] = following[l * RHS : (l + 1) * RHS]
-
         def add_forward(step, sofar):
             for i in range(STRIDE):
                 e = step * STRIDE + i
@@ -420,7 +387,53 @@
                 sofar = sofar + nt(spread, near[e])
             return sofar
 
-        total = lax.fori_loop(0, CAPACITY // STRIDE, add_forward, total)
+        fill_group(0)
+        send_group(0)
+
+        fill_group(1)
+        exact = finish_vector(n)
+        rounded = [value.astype(BF16) for value in exact]
+        x_out[n] = jnp.concatenate(exact, axis=0).astype(BF16)
+        for l in range(LEAVES):
+            extended[l] = rounded[l].astype(F32)
+        x_copy(n).start()
+        send_group(1)
+
+        @pl.when(n > 0)
+        def _():
+            out_copy(n - 1).start()
+
+        fill_group(2)
+        backward = add_backward(0, jnp.zeros((2 * LEAVES * RHS, POINTS), F32))
+        send_group(2)
+
+        fill_group(3)
+        backward = add_backward(2, add_backward(1, backward))
+        send_group(3)
+
+        fill_group(4)
+        backward = add_backward(3, backward)
+        near_out[n] = backward[LEAVES * RHS :].astype(BF16)
+        near_copy(n).start()
+        send_group(4)
+
+        fill_group(5)
+        total = backward[: LEAVES * RHS] + jnp.concatenate(
+            [nn(rounded[l], diag[l]) for l in range(LEAVES)], axis=0
+        )
+        x_copy(n).wait_recv()
+        following = x_in[n].astype(F32)
+        for l in range(LEAVES):
+            extended[LEAVES + l] = following[l * RHS : (l + 1) * RHS]
+        total = add_forward(0, total)
+        send_group(5)
+
+        fill(leaf_rows, leaf_twice, leaf_w, leaf_slots, 0, leaf_pairs, store_leaf)
+        total = add_forward(1, total)
+        for v in range(CLOSE):
+            if v != REACH:
+                leaf_copy(n, v).start()
+        total = add_forward(3, add_forward(2, total))
 
         def take(box, w, slots, first_slot, slot_count, pairs, sofar):
             through, handed = sofar

time: 51.9 us -> 64.5 us (1.24)
  Pallas kernels: 49 us -> 62.1 us
    pallas_call x1, Pallas kernels: 49 us -> 62.1 us  [on_device(): pl.pallas_call(functools.partial(kernel, devices), out_shape=jax.ShapeDty...]
where the time goes in v12:
time: 64.5 us; the launch traced here: 64.3 us
  Pallas kernels  62.1 us (96%)
  local copies, waits for them, and re-layouts  1.57 us (2%)
  between operations  0.66 us (1%)
    pallas_call x1, Pallas kernels, on_device(): pl.pallas_call(functools.partial(kernel, devices), out_shape=jax.ShapeDty...  62.1 us
    unnamed x1, local copies, waits for them, and re-layouts  1.57 us

profile of v12, /device:TPU:1, one launch (start us, length us, event | category | flops | bytes accessed | tf_op | source)
XLA Modules:
  0.0 64.3 jit_solution(9347095088398093953)
XLA Ops:
  0.7 62.1 %h2_products.1 = f32[4,4,8,256]{3,2,1,0:T(8,128)} custom-call(f32[4,8,256]{2,1,0:T(8,128)} %start_hbm.1, s32[4]{0:T(128)} %leaf_size.1, bf16[4,256,256]{2,1,0:T(8,128)(2,1)} %diag_hbm.1, bf16[16,256,256]{2,1,0:T(8,128)(2,1)} %near_hbm.1, s32[1]{0:T(128)S(6)} %copy.14.near_count, s32[16]{0:T(128)} %near_first.1, s32[16]{0:T(128)} %near_second.1, ...), custom_call_target="tpu_custom_call" | custom-call | tf_op jit(solution)/shard_map/h2_products/pallas_call | solution.py:532
  62.8 1.6 %copy.15 = f32[4,4,8,256]{3,2,1,0:T(8,128)} copy(f32[4,4,8,256]{3,2,1,0:T(8,128)} %h2_products.1) | data formatting | bytes 262144
